TPU v7x, 32 devices: a whole 2x2x4 slice. The times are simulated.
32 devices in a mesh: rows: 8 (over z, x), head: 4 (over y, core).
Axes of the slice: x: 2, y: 2, z: 4, core: 2. Of those that a mesh axis runs over, the one named last changes fastest.
Arguments:
- media: bfloat16 [32, 256, 1536], P('rows', 'head'), may hold values from -6 to 6
- latents: bfloat16 [32, 64, 1536], P('rows', 'head'), may hold values from -6 to 6
- counts: int32 [4], replicated, may hold values from 1 to 8, 20 in all
- media_gain: float32 [1536], replicated, may hold values from 0.1 to 1.9
- media_shift: float32 [1536], replicated, may hold values from -1.5 to 1.5
- latent_gain: float32 [1536], replicated, may hold values from 0.1 to 1.9
- latent_shift: float32 [1536], replicated, may hold values from -1.5 to 1.5
- w_query: bfloat16 [1536, 1536], replicated, may hold values from -0.15625 to 0.15625
- w_key: bfloat16 [1536, 1536], replicated, may hold values from -0.15625 to 0.15625
- w_value: bfloat16 [1536, 1536], replicated, may hold values from -0.15625 to 0.15625
- w_out: bfloat16 [1536, 1536], replicated, may hold values from -1.25 to 1.25
- ffn_gain: float32 [1536], replicated, may hold values from 0.1 to 1.9
- ffn_shift: float32 [1536], replicated, may hold values from -1.5 to 1.5
- w_up: bfloat16 [1536, 6144], replicated, may hold values from -0.15625 to 0.15625
- w_down: bfloat16 [6144, 1536], replicated, may hold values from -0.078125 to 0.078125
- cotangent: bfloat16 [32, 64, 1536], P('rows', 'head'), may hold values from -6 to 6
Outputs:
- latents_out: float32 [32, 64, 1536], P('rows', 'head')
- media_grad: float32 [32, 256, 1536], P('rows', 'head')
- latents_grad: float32 [32, 64, 1536], P('rows', 'head')
- media_gain_grad: float32 [1536], P(('rows', 'head'))
- media_shift_grad: float32 [1536], P(('rows', 'head'))
- latent_gain_grad: float32 [1536], P(('rows', 'head'))
- latent_shift_grad: float32 [1536], P(('rows', 'head'))
- query_grad: float32 [1536, 1536], P('rows', 'head')
- key_grad: float32 [1536, 1536], P('rows', 'head')
- value_grad: float32 [1536, 1536], P('rows', 'head')
- out_grad: float32 [1536, 1536], P('rows', 'head')
- ffn_gain_grad: float32 [1536], P(('rows', 'head'))
- ffn_shift_grad: float32 [1536], P(('rows', 'head'))
- up_grad: float32 [1536, 6144], P('rows', 'head')
- down_grad: float32 [6144, 1536], P('head', 'rows')
Inputs may be any that keep to these rules, and one draw needn't show every extreme that they name: At most 8 images in a sequence, and some sequence has exactly 8; the counts sum to 20.
All inputs are finite; a program needn't handle non-finite values.
Results may differ from a plain program's by a relative error of at most 0.017.
Values may be sent and summed in bfloat16 or wider, within the bound.
A program may use at most 192 MiB of HBM per device.

v0:
```python
import math

import jax
import jax.numpy as jnp
from jax import lax
from jax.sharding import PartitionSpec as P

HEAD_DIM = 96
MAX_IMG = 8


epsilon = 1e-05


def standardize(values):
    row_mean = jnp.mean(values, axis=-1, keepdims=True)
    centered = values - row_mean
    variance = jnp.mean(centered * centered, axis=-1, keepdims=True)
    inv_scale = lax.rsqrt(variance + epsilon)
    return (centered * inv_scale, inv_scale)


def norm_back(d_scaled, normed, inv_scale):
    first_mean = jnp.mean(d_scaled, axis=-1, keepdims=True)
    second_mean = jnp.mean(d_scaled * normed, axis=-1, keepdims=True)
    return inv_scale * (d_scaled - first_mean - normed * second_mean)


def split_heads(array_in):
    return array_in.reshape(
        array_in.shape[0], array_in.shape[1], array_in.shape[2] // HEAD_DIM, HEAD_DIM
    )


def attend(query, keys, values):
    images, lat_rows, feature_width = query.shape
    score_scale = 1.0 / math.sqrt(HEAD_DIM)
    scores = (
        jnp.einsum(
            "iqhe,ikhe->ihqk",
            split_heads(query),
            split_heads(keys),
            preferred_element_type=jnp.float32,
        )
        * score_scale
    )
    row_max = jnp.max(scores, axis=-1, keepdims=True)
    row_total = jnp.sum(jnp.exp(scores - row_max), axis=-1, keepdims=True)
    log_total = row_max + jnp.log(row_total)
    attn_probs = jnp.exp(scores - log_total).astype(jnp.bfloat16)
    mixed = jnp.einsum(
        "ihqk,ikhe->iqhe", attn_probs, split_heads(values), preferred_element_type=jnp.float32
    )
    return (mixed.reshape(images, lat_rows, feature_width).astype(jnp.bfloat16), log_total)


def attend_back(query, keys, values, log_total, d_mixed):
    images, lat_rows, feature_width = query.shape
    score_scale = 1.0 / math.sqrt(HEAD_DIM)
    query_heads = split_heads(query)
    key_heads = split_heads(keys)
    value_heads = split_heads(values)
    d_heads = split_heads(d_mixed)
    scores = (
        jnp.einsum("iqhe,ikhe->ihqk", query_heads, key_heads, preferred_element_type=jnp.float32)
        * score_scale
    )
    recomputed = jnp.exp(scores - log_total)
    d_probs = jnp.einsum(
        "iqhe,ikhe->ihqk", d_heads, value_heads, preferred_element_type=jnp.float32
    )
    d_scores = (
        recomputed * (d_probs - jnp.sum(recomputed * d_probs, axis=-1, keepdims=True))
    ).astype(jnp.bfloat16)
    d_query = (
        jnp.einsum("ihqk,ikhe->iqhe", d_scores, key_heads, preferred_element_type=jnp.float32)
        * score_scale
    )
    d_keys = (
        jnp.einsum("ihqk,iqhe->ikhe", d_scores, query_heads, preferred_element_type=jnp.float32)
        * score_scale
    )
    d_values = jnp.einsum(
        "ihqk,iqhe->ikhe",
        recomputed.astype(jnp.bfloat16),
        d_heads,
        preferred_element_type=jnp.float32,
    )
    key_count = keys.shape[1]
    return (
        d_query.reshape(images, lat_rows, feature_width).astype(jnp.bfloat16),
        d_keys.reshape(images, key_count, feature_width).astype(jnp.bfloat16),
        d_values.reshape(images, key_count, feature_width).astype(jnp.bfloat16),
    )


def image_mask(counts, group_size):
    first_image = lax.axis_index("rows") * group_size
    image_ids = first_image + jnp.arange(group_size, dtype=jnp.int32)
    sequence = image_ids // MAX_IMG
    slot_ids = image_ids % MAX_IMG
    seq_table = jnp.arange(counts.shape[0], dtype=jnp.int32)
    seq_limit = jnp.sum(
        jnp.where(sequence[:, None] == seq_table[None, :], counts[None, :], 0), axis=1
    )
    return (slot_ids < seq_limit).astype(jnp.float32)


def body(
    media,
    latents,
    counts,
    media_gain,
    media_shift,
    latent_gain,
    latent_shift,
    w_query,
    w_key,
    w_value,
    w_out,
    ffn_gain,
    ffn_shift,
    w_up,
    w_down,
    cotangent,
):
    group_size = media.shape[0]
    patch_rows = media.shape[1]
    lat_local = latents.shape[1]
    head_count = lax.axis_size("head")
    latents_wide = latents.astype(jnp.float32)
    media_hat, media_scale = standardize(media.astype(jnp.float32))
    latent_hat, latent_scale = standardize(latents_wide)
    media_norm = (media_hat * media_gain + media_shift).astype(jnp.bfloat16)
    latent_norm = (latent_hat * latent_gain + latent_shift).astype(jnp.bfloat16)
    query = jnp.einsum(
        "ild,de->ile", latent_norm, w_query, preferred_element_type=jnp.float32
    ).astype(jnp.bfloat16)
    key_rows = jnp.concatenate([media_norm, latent_norm], axis=1)
    keys = jnp.einsum("ikd,de->ike", key_rows, w_key, preferred_element_type=jnp.float32).astype(
        jnp.bfloat16
    )
    values = jnp.einsum(
        "ikd,de->ike", key_rows, w_value, preferred_element_type=jnp.float32
    ).astype(jnp.bfloat16)
    query_att, keys_att, values_att = (
        lax.all_to_all(query, "head", split_axis=2, concat_axis=1, tiled=True),
        lax.all_to_all(keys, "head", split_axis=2, concat_axis=1, tiled=True),
        lax.all_to_all(values, "head", split_axis=2, concat_axis=1, tiled=True),
    )
    mixed_att, log_total = attend(query_att, keys_att, values_att)
    mixed = lax.all_to_all(mixed_att, "head", split_axis=1, concat_axis=2, tiled=True)
    residual = latents_wide + jnp.einsum(
        "ild,de->ile", mixed, w_out, preferred_element_type=jnp.float32
    )
    ffn_hat, ffn_scale = standardize(residual)
    ffn_norm = (ffn_hat * ffn_gain + ffn_shift).astype(jnp.bfloat16)
    hidden = jnp.einsum("ild,df->ilf", ffn_norm, w_up, preferred_element_type=jnp.float32)
    activated_wide, gelu_pull = jax.vjp(jax.nn.gelu, hidden)
    activated = activated_wide.astype(jnp.bfloat16)
    output = residual + jnp.einsum(
        "ilf,fd->ild", activated, w_down, preferred_element_type=jnp.float32
    )
    live_mask = image_mask(counts, group_size)
    d_out = (cotangent.astype(jnp.float32) * live_mask[:, None, None]).astype(jnp.bfloat16)
    d_activated = jnp.einsum("ild,fd->ilf", d_out, w_down, preferred_element_type=jnp.float32)
    d_hidden = gelu_pull(d_activated)[0].astype(jnp.bfloat16)
    d_ffn_norm = jnp.einsum("ilf,df->ild", d_hidden, w_up, preferred_element_type=jnp.float32)
    ffn_gain_part = jnp.sum(d_ffn_norm * ffn_hat, axis=(0, 1))
    ffn_shift_part = jnp.sum(d_ffn_norm, axis=(0, 1))
    ffn_norm_all, d_out_all = (
        lax.all_gather(ffn_norm, "head", axis=1, tiled=True),
        lax.all_gather(d_out, "head", axis=1, tiled=True),
    )
    d_hidden_cols, activated_cols = (
        lax.all_to_all(d_hidden, "head", split_axis=2, concat_axis=1, tiled=True),
        lax.all_to_all(activated, "head", split_axis=2, concat_axis=1, tiled=True),
    )
    up_part = jnp.einsum(
        "ild,ilf->df", ffn_norm_all, d_hidden_cols, preferred_element_type=jnp.float32
    )
    down_part = jnp.einsum(
        "ilf,ild->fd", activated_cols, d_out_all, preferred_element_type=jnp.float32
    )
    d_residual = d_out.astype(jnp.float32) + norm_back(d_ffn_norm * ffn_gain, ffn_hat, ffn_scale)
    d_attn = d_residual.astype(jnp.bfloat16)
    d_mixed = jnp.einsum("ile,de->ild", d_attn, w_out, preferred_element_type=jnp.float32).astype(
        jnp.bfloat16
    )
    d_mixed_att = lax.all_to_all(d_mixed, "head", split_axis=2, concat_axis=1, tiled=True)
    d_triple = attend_back(query_att, keys_att, values_att, log_total, d_mixed_att)
    d_query, d_keys, d_values = (
        lax.all_to_all(d_triple[0], "head", split_axis=1, concat_axis=2, tiled=True),
        lax.all_to_all(d_triple[1], "head", split_axis=1, concat_axis=2, tiled=True),
        lax.all_to_all(d_triple[2], "head", split_axis=1, concat_axis=2, tiled=True),
    )
    d_query_cols, d_keys_cols, d_values_cols = d_triple
    d_attn_cols = lax.all_to_all(d_attn, "head", split_axis=2, concat_axis=1, tiled=True)
    key_rows_all, mixed_all = (
        lax.all_gather(key_rows, "head", axis=1, tiled=True),
        lax.all_gather(mixed, "head", axis=1, tiled=True),
    )
    feature_width = key_rows.shape[2]
    latent_norm_all = key_rows_all.reshape(
        group_size, head_count, patch_rows + lat_local, feature_width
    )[:, :, patch_rows:]
    latent_norm_all = latent_norm_all.reshape(group_size, head_count * lat_local, feature_width)
    query_part = jnp.einsum(
        "ild,ile->de", latent_norm_all, d_query_cols, preferred_element_type=jnp.float32
    )
    key_part = jnp.einsum(
        "ikd,ike->de", key_rows_all, d_keys_cols, preferred_element_type=jnp.float32
    )
    value_part = jnp.einsum(
        "ikd,ike->de", key_rows_all, d_values_cols, preferred_element_type=jnp.float32
    )
    out_part = jnp.einsum("ild,ile->de", mixed_all, d_attn_cols, preferred_element_type=jnp.float32)
    d_key_rows = jnp.einsum("ike,de->ikd", d_keys, w_key, preferred_element_type=jnp.float32)
    d_key_rows = d_key_rows + jnp.einsum(
        "ike,de->ikd", d_values, w_value, preferred_element_type=jnp.float32
    )
    d_media_norm = d_key_rows[:, :patch_rows]
    d_latent_norm = d_key_rows[:, patch_rows:] + jnp.einsum(
        "ile,de->ild", d_query, w_query, preferred_element_type=jnp.float32
    )
    media_gain_part = jnp.sum(d_media_norm * media_hat, axis=(0, 1))
    media_shift_part = jnp.sum(d_media_norm, axis=(0, 1))
    latent_gain_part = jnp.sum(d_latent_norm * latent_hat, axis=(0, 1))
    latent_shift_part = jnp.sum(d_latent_norm, axis=(0, 1))
    media_grad = norm_back(d_media_norm * media_gain, media_hat, media_scale)
    latents_grad = d_residual + norm_back(d_latent_norm * latent_gain, latent_hat, latent_scale)
    norm_sums = (
        lax.psum_scatter(media_gain_part, ("rows", "head"), scatter_dimension=0, tiled=True),
        lax.psum_scatter(media_shift_part, ("rows", "head"), scatter_dimension=0, tiled=True),
        lax.psum_scatter(latent_gain_part, ("rows", "head"), scatter_dimension=0, tiled=True),
        lax.psum_scatter(latent_shift_part, ("rows", "head"), scatter_dimension=0, tiled=True),
        lax.psum_scatter(ffn_gain_part, ("rows", "head"), scatter_dimension=0, tiled=True),
        lax.psum_scatter(ffn_shift_part, ("rows", "head"), scatter_dimension=0, tiled=True),
    )
    query_sum, key_sum, value_sum, out_sum, up_sum, down_sum = (
        lax.psum_scatter(
            query_part.astype(jnp.bfloat16), "rows", scatter_dimension=0, tiled=True
        ).astype(jnp.float32),
        lax.psum_scatter(
            key_part.astype(jnp.bfloat16), "rows", scatter_dimension=0, tiled=True
        ).astype(jnp.float32),
        lax.psum_scatter(
            value_part.astype(jnp.bfloat16), "rows", scatter_dimension=0, tiled=True
        ).astype(jnp.float32),
        lax.psum_scatter(
            out_part.astype(jnp.bfloat16), "rows", scatter_dimension=0, tiled=True
        ).astype(jnp.float32),
        lax.psum_scatter(
            up_part.astype(jnp.bfloat16), "rows", scatter_dimension=0, tiled=True
        ).astype(jnp.float32),
        lax.psum_scatter(
            down_part.astype(jnp.bfloat16), "rows", scatter_dimension=1, tiled=True
        ).astype(jnp.float32),
    )
    return (
        output,
        media_grad,
        latents_grad,
        norm_sums[0],
        norm_sums[1],
        norm_sums[2],
        norm_sums[3],
        query_sum,
        key_sum,
        value_sum,
        out_sum,
        norm_sums[4],
        norm_sums[5],
        up_sum,
        down_sum,
    )


def solution(mesh):
    return jax.shard_map(
        body,
        mesh=mesh,
        in_specs=(
            P("rows", "head", None),
            P("rows", "head", None),
            P(),
            P(),
            P(),
            P(),
            P(),
            P(),
            P(),
            P(),
            P(),
            P(),
            P(),
            P(),
            P(),
            P("rows", "head", None),
        ),
        out_specs=(
            P("rows", "head", None),
            P("rows", "head", None),
            P("rows", "head", None),
            P(("rows", "head")),
            P(("rows", "head")),
            P(("rows", "head")),
            P(("rows", "head")),
            P("rows", "head"),
            P("rows", "head"),
            P("rows", "head"),
            P("rows", "head"),
            P(("rows", "head")),
            P(("rows", "head")),
            P("rows", "head"),
            P("head", "rows"),
        ),
        check_vma=False,
    )
```

profile of v0, /device:TPU:0, one launch (start us, length us, event | category | flops | bytes accessed | tf_op | source)
XLA Modules:
  0.0 655.6 jit_solution(8025977481341338659)
XLA Ops:
  11.9 3.3 fusion.46
  16.2 2.3 reshape.198
  18.5 4.2 all-to-all-start.1
  24.4 4.0 fusion.31
  28.5 2.2 copy.103
  30.7 3.6 all-to-all-start
  34.2 5.0 fusion.34
  39.2 3.5 copy.107
  42.7 11.6 %all-to-all-done = bf16[4,80,1536]{1,0,2:T(4,128)(2,1)S(1)} async-done(((bf16[4,80,1536]{1,0,2:T(4,128)(2,1)}), bf16[4,80,1536]{1,0,2:T(4,128)(2,1)S(1)}, u32[]{:S(2)}, u32[]{:S(2)}) %all-to-all-start) | async-done | bytes 983072 | tf_op jit(solution)/shard_map/all_to_all | solution.py:149
  54.3 4.4 all-to-all-start.2
  62.2 2.6 copy.106
  69.1 15.0 %all-to-all-done.2 = bf16[4,80,1536]{1,0,2:T(4,128)(2,1)} async-done(((bf16[4,80,1536]{1,0,2:T(4,128)(2,1)}), bf16[4,80,1536]{1,0,2:T(4,128)(2,1)}, u32[]{:S(2)}, u32[]{:S(2)}) %all-to-all-start.2) | async-done | bytes 983072 | tf_op jit(solution)/shard_map/all_to_all | solution.py:148
  84.1 3.5 copy.108
  87.6 2.9 reshape.181
  90.5 2.4 copy.110
  97.2 3.6 all-to-all-start.3
  102.5 3.6 all-to-all-done.3
  106.2 3.4 fusion.102
  110.1 11.7 %multiply_convert_fusion.2 = (bf16[4,16,6144]{2,1,0:T(8,128)(2,1)}, f32[4,16,6144]{2,1,0:T(8,128)}) fusion(bf16[4,16,1536]{2,1,0:T(8,128)(2,1)S(1)} %add_convert_fusion, bf16[1536,6144]{1,0:T(8,128)(2,1)} %param.29), kind=kOutput, calls=%fused_computation.69 | convolution fusion | flops 1211498496 | bytes 21430272 | tf_op jit(solution)/shard_map/ild,df->ilf/dot_general | solution.py:158
  121.7 12.7 %fusion.71 = bf16[4,16,6144]{2,1,0:T(8,128)(2,1)S(1)} fusion(f32[4,16,6144]{2,1,0:T(8,128)} %get-tuple-element.38, bf16[4,16,1536]{2,1,0:T(8,128)(2,1)} %multiply_convert_fusion.3, bf16[6144,1536]{1,0:T(8,128)(2,1)} %param.30), kind=kOutput, calls=%fused_computation.66 | convolution fusion | flops 1215823872 | bytes 21430272 | tf_op jit(solution)/shard_map/ild,fd->ilf/dot_general | solution.py:166
  134.5 13.6 %multiply_reduce_fusion.1 = (f32[1536]{0:T(1024)}, f32[4,16]{1,0:T(4,128)}, f32[4,16]{1,0:T(4,128)}, f32[1536]{0:T(1024)}, f32[4,16,1536]{2,1,0:T(8,128)}) fusion(f32[4,16,1536]{2,1,0:T(8,128)S(1)} %get-tuple-element.36, f32[4,16]{1,0:T(4,128)} %copy-done.26, f32[4,16]{1,0:T(4,128)} %copy-done.21, f32[1536]{0:T(1024)S(1)} %copy-done.18, ...), kind=kOutput, calls=%fused_computation.100 | convolution fusion | flops 1208841216 | bytes 20466688 | tf_op jit(solution)/shard_map/ilf,df->ild/dot_general | solution.py:168
  151.3 3.1 copy.134
  154.4 4.3 reshape.202
  158.7 4.0 all-to-all-start.8
  162.7 11.0 %all_gather.13 = bf16[4,64,1536]{2,1,0:T(8,128)(2,1)} all-gather(bf16[4,16,1536]{2,1,0:T(8,128)(2,1)} %bitcast.201), channel_id=1, replica_groups=mesh['rows'=8,'head'=4] {'head'}, dimensions={1}, use_global_device_ids=true | all-gather | bytes 983040 | tf_op jit(solution)/shard_map/all_gather | solution.py:201
  173.7 4.2 reshape.203
  177.9 3.2 copy.135
  181.1 2.8 fusion.28
  184.0 4.7 fusion.49
  188.6 3.1 copy.116
  191.7 3.9 reshape.200
  195.6 9.6 %all_to_all.186 = bf16[4,2,12288]{2,1,0:T(2,128)(2,1)} all-to-all(bf16[4,2,12288]{2,1,0:T(2,128)(2,1)} %reshape.200), channel_id=1, replica_groups=mesh['rows'=8,'head'=4] {'head'}, dimensions={0} | all-to-all | bytes 393216 | tf_op jit(solution)/shard_map/all_to_all | solution.py:190
  205.2 4.2 reshape.201
  209.4 3.2 copy.117
  227.0 5.8 fusion.29
  235.5 5.9 fusion.30
  241.5 6.5 copy.136
  248.0 8.5 %reshape.204 = bf16[4,2,49152]{2,1,0:T(2,128)(2,1)} reshape(bf16[6144,4,16]{2,1,0:T(4,128)(2,1)} %bitcast.180) | data formatting | bytes 1572864
  256.5 3.7 all-to-all-start.9
  260.2 16.7 %all_gather.14 = bf16[4,64,1536]{2,1,0:T(8,128)(2,1)S(1)} all-gather(bf16[4,16,1536]{2,1,0:T(8,128)(2,1)S(1)} %copy-done.14), channel_id=1, replica_groups=mesh['rows'=8,'head'=4] {'head'}, dimensions={1}, use_global_device_ids=true | all-gather | bytes 983040 | tf_op jit(solution)/shard_map/all_gather | solution.py:172
  276.9 5.6 reshape.205
  282.5 8.1 %copy.137 = bf16[4,16,4,1536]{3,1,2,0:T(8,128)(2,1)S(1)} copy(bf16[4,16,4,1536]{1,0,3,2:T(4,128)(2,1)} %bitcast.181) | data formatting | bytes 1572864 | tf_op jit(solution)/shard_map/all_to_all | solution.py:176
  290.6 3.6 bitcast_convert_fusion.1
  295.4 6.2 copy.138
  301.6 8.5 %reshape.206 = bf16[4,2,49152]{2,1,0:T(2,128)(2,1)} reshape(bf16[6144,4,16]{2,1,0:T(4,128)(2,1)} %bitcast.183) | data formatting | bytes 1572864
  310.1 3.5 all-to-all-start.10
  313.6 16.7 %all_gather.15 = bf16[4,64,1536]{2,1,0:T(8,128)(2,1)S(1)} all-gather(bf16[4,16,1536]{2,1,0:T(8,128)(2,1)} %multiply_convert_fusion.3), channel_id=1, replica_groups=mesh['rows'=8,'head'=4] {'head'}, dimensions={1}, use_global_device_ids=true | all-gather | bytes 983040 | tf_op jit(solution)/shard_map/all_gather | solution.py:173
  330.3 5.6 reshape.207
  335.9 8.2 %copy.139 = bf16[4,16,4,1536]{3,1,2,0:T(8,128)(2,1)S(1)} copy(bf16[4,16,4,1536]{1,0,3,2:T(4,128)(2,1)} %bitcast.182) | data formatting | bytes 1572864 | tf_op jit(solution)/shard_map/all_to_all | solution.py:177
  344.1 3.6 bitcast_convert_fusion
  349.5 3.4 all-to-all-start.7
  352.9 3.3 copy.121
  358.2 4.2 all-to-all-start.5
  362.4 3.3 copy.125
  365.7 10.5 %all-to-all-done.5 = bf16[4,320,384]{2,0,1:T(4,128)(2,1)} async-done(((bf16[4,320,384]{2,0,1:T(4,128)(2,1)}), bf16[4,320,384]{2,0,1:T(4,128)(2,1)}, u32[]{:S(2)}, u32[]{:S(2)}) %all-to-all-start.5) | async-done | bytes 983072 | tf_op jit(solution)/shard_map/all_to_all | solution.py:194
  376.2 4.5 all-to-all-start.6
  380.8 10.5 %fusion.43 = f32[4,16,1536]{2,1,0:T(8,128)} fusion(f32[4,16,1536]{2,1,0:T(8,128)S(1)} %get-tuple-element.36, bf16[4,16,6144]{2,1,0:T(8,128)(2,1)S(1)} %copy-done.3, bf16[6144,1536]{1,0:T(8,128)(2,1)} %param.30), kind=kOutput, calls=%fused_computation.40 | convolution fusion | flops 1208057856 | bytes 20447232 | tf_op jit(solution)/shard_map/ilf,fd->ild/dot_general | solution.py:161
  396.0 4.2 fusion.12
  400.3 4.2 fusion.24
  407.6 41.8 %all-reduce.6 = (f32[1536]{0:T(1024)S(1)}, f32[1536]{0:T(1024)S(1)}, f32[1536]{0:T(1024)S(1)}, f32[1536]{0:T(1024)S(1)}, f32[1536]{0:T(1024)S(1)}, /*index=5*/f32[1536]{0:T(1024)S(1)}) all-reduce(f32[1536]{0:T(1024)S(1)} %get-tuple-element.15, ...), channel_id=2, replica_groups=mesh['rows'=8,'head'=4] {'rows','head'}, use_global_device_ids=true, to_apply=%region_17.18.clone | all-reduce | flops 9216 | bytes 73728
  462.4 84.6 %reduce-scatter.15.cloned.1.call-done = bf16[192,1536]{1,0:T(8,128)(2,1)} async-done(((bf16[1536,1536]{1,0:T(8,128)(2,1)}), bf16[192,1536]{1,0:T(8,128)(2,1)}) %reduce-scatter.15.cloned.1.call-update) | async-done | bytes 589840 | tf_op jit(solution)/shard_map/reduce_scatter | solution.py:253
  547.0 2.2 convert_element_type.172
  549.2 96.3 %reduce-scatter.17.cloned.1.call-done = bf16[1536,192]{0,1:T(8,128)(2,1)} async-done(((bf16[1536,1536]{0,1:T(8,128)(2,1)}), bf16[1536,192]{0,1:T(8,128)(2,1)}) %reduce-scatter.17.cloned.1.call-update) | async-done | bytes 589840 | tf_op jit(solution)/shard_map/reduce_scatter | solution.py:256
  645.5 2.2 convert_element_type.174
  (190 shorter events, 66.7 us)
Async XLA Ops:
  9.1 1.1 copy-start.28
  10.2 0.6 copy-start.34
  15.1 7.6 %copy-start = (bf16[4,64,1536]{2,1,0:T(8,128)(2,1)S(1)}, bf16[4,64,1536]{2,1,0:T(8,128)(2,1)}, u32[]{:S(2)}) copy-start(bf16[4,64,1536]{2,1,0:T(8,128)(2,1)} %param.16) | copy-start | bytes 2359300
  16.2 7.9 %copy-start.19 = (f32[1536]{0:T(1024)S(1)}, f32[1536]{0:T(1024)}, u32[]{:S(2)}) copy-start(f32[1536]{0:T(1024)} %param.19) | copy-start | bytes 18436
  16.2 7.9 %copy-start.40 = (f32[1536]{0:T(1024)S(1)}, f32[1536]{0:T(1024)}, u32[]{:S(2)}) copy-start(f32[1536]{0:T(1024)} %param.20) | copy-start | bytes 18436
  18.5 12.2 %all-to-all-start.1 = ((bf16[4,2,12288]{2,1,0:T(2,128)(2,1)}), bf16[4,2,12288]{2,1,0:T(2,128)(2,1)S(1)}, u32[]{:S(2)}, u32[]{:S(2)}) async-start(bf16[4,2,12288]{2,1,0:T(2,128)(2,1)} %reshape.198), calls=%async_computation.1 | async-start | bytes 393216 | tf_op jit(solution)/shard_map/all_to_all | solution.py:147
  22.9 0.6 copy-start.24
  23.5 0.6 copy-start.30
  30.7 23.6 %all-to-all-start = ((bf16[4,80,1536]{1,0,2:T(4,128)(2,1)}), bf16[4,80,1536]{1,0,2:T(4,128)(2,1)S(1)}, u32[]{:S(2)}, u32[]{:S(2)}) async-start(bf16[4,80,1536]{1,0,2:T(4,128)(2,1)} %copy.103), calls=%async_computation | async-start | bytes 3145728 | tf_op jit(solution)/shard_map/all_to_all | solution.py:149
  54.3 29.8 %all-to-all-start.2 = ((bf16[4,80,1536]{1,0,2:T(4,128)(2,1)}), bf16[4,80,1536]{1,0,2:T(4,128)(2,1)}, u32[]{:S(2)}, u32[]{:S(2)}) async-start(bf16[4,80,1536]{1,0,2:T(4,128)(2,1)} %copy.107), calls=%async_computation.2 | async-start | bytes 3145728 | tf_op jit(solution)/shard_map/all_to_all | solution.py:148
  58.7 1.1 copy-start.44
  58.7 162.6 %all-gather.2.cloned.1.call-start = ((), (), s32[]{:S(2)}) async-start(), calls=%async_computation.17 | async-start | bytes 4915200 | tf_op jit(solution)/shard_map/all_gather | solution.py:200
  60.0 40.8 %copy-start.42 = (f32[4]{0:T(128)}, f32[4]{0:T(128)S(1)}, u32[]{:S(2)}) copy-start(f32[4]{0:T(128)S(1)} %compare_convert_fusion) | copy-start | bytes 52
  69.1 26.2 %copy-start.1 = (bf16[4,320,4,96]{1,3,2,0:T(8,128)(2,1)}, bf16[4,320,4,96]{1,3,2,0:T(8,128)(2,1)S(1)}, u32[]{:S(2)}) copy-start(bf16[4,320,4,96]{1,3,2,0:T(8,128)(2,1)S(1)} %copy.111) | copy-start | bytes 2949124
  96.1 10.1 %copy-start.4 = (bf16[4,16,1536]{2,1,0:T(8,128)(2,1)S(1)}, bf16[4,16,1536]{2,1,0:T(8,128)(2,1)}, u32[]{:S(2)}) copy-start(bf16[4,16,1536]{2,1,0:T(8,128)(2,1)} %param.17) | copy-start | bytes 589828
  97.2 8.9 %all-to-all-start.3 = ((bf16[4,64,384]{2,0,1:T(4,128)(2,1)}), bf16[4,64,384]{2,0,1:T(4,128)(2,1)S(1)}, u32[]{:S(2)}, u32[]{:S(2)}) async-start(bf16[4,64,384]{2,0,1:T(4,128)(2,1)} %reshape.197), calls=%async_computation.3 | async-start | bytes 393216 | tf_op jit(solution)/shard_map/all_to_all | solution.py:152
  106.2 3.5 copy-start.12
  106.2 3.7 copy-start.18
  106.2 3.7 copy-start.41
  109.7 12.0 %copy-start.21 = (f32[4,16]{1,0:T(4,128)}, f32[4,16]{1,0:T(4,128)S(1)}, u32[]{:S(2)}) copy-start(f32[4,16]{1,0:T(4,128)S(1)} %broadcast_multiply_fusion.4) | copy-start | bytes 772
  109.9 11.8 %copy-start.26 = (f32[4,16]{1,0:T(4,128)}, f32[4,16]{1,0:T(4,128)S(1)}, u32[]{:S(2)}) copy-start(f32[4,16]{1,0:T(4,128)S(1)} %add_rsqrt_fusion) | copy-start | bytes 772
  110.1 11.7 %copy-start.13 = (bf16[4,16,1536]{2,1,0:T(8,128)(2,1)}, bf16[4,16,1536]{2,1,0:T(8,128)(2,1)S(1)}, u32[]{:S(2)}) copy-start(bf16[4,16,1536]{2,1,0:T(8,128)(2,1)S(1)} %add_convert_fusion) | copy-start | bytes 589828
  148.7 0.6 copy-start.36
  148.7 0.6 copy-start.38
  158.7 15.0 %all-to-all-start.8 = ((bf16[4,2,12288]{2,1,0:T(2,128)(2,1)}), bf16[4,2,12288]{2,1,0:T(2,128)(2,1)}, u32[]{:S(2)}, u32[]{:S(2)}) async-start(bf16[4,2,12288]{2,1,0:T(2,128)(2,1)} %reshape.202), calls=%async_computation.11 | async-start | bytes 393216 | tf_op jit(solution)/shard_map/all_to_all | solution.py:198
  162.7 293.1 %reduce-scatter.13.cloned.1.call-start = ((), (), s32[]{:S(2)}) async-start(), calls=%async_computation.21 | async-start | bytes 1327104 | tf_op jit(solution)/shard_map/reduce_scatter | solution.py:250
  183.9 273.5 %reduce-scatter.7.cloned.1.call-start = ((), (), s32[]{:S(2)}) async-start(), calls=%async_computation.18 | async-start | bytes 1327104 | tf_op jit(solution)/shard_map/reduce_scatter | solution.py:241
  216.4 1.3 copy-start.2
  217.7 0.9 copy-start.6
  221.3 1.2 copy-start.16
  224.2 234.8 %reduce-scatter.9.cloned.1.call-start = ((), (), s32[]{:S(2)}) async-start(), calls=%async_computation.19 | async-start | bytes 1327104 | tf_op jit(solution)/shard_map/reduce_scatter | solution.py:244
  226.0 1.0 copy-start.9
  232.9 227.8 %reduce-scatter.11.cloned.1.call-start = ((), (), s32[]{:S(2)}) async-start(), calls=%async_computation.20 | async-start | bytes 1327104 | tf_op jit(solution)/shard_map/reduce_scatter | solution.py:247
  234.5 1.0 copy-start.10
  256.5 3.7 copy-start.14
  256.5 20.4 %all-to-all-start.9 = ((bf16[4,2,49152]{2,1,0:T(2,128)(2,1)}), bf16[4,2,49152]{2,1,0:T(2,128)(2,1)S(1)}, u32[]{:S(2)}, u32[]{:S(2)}) async-start(bf16[4,2,49152]{2,1,0:T(2,128)(2,1)} %reshape.204), calls=%async_computation.13 | async-start | bytes 1572864 | tf_op jit(solution)/shard_map/all_to_all | solution.py:176
  260.1 286.9 %reduce-scatter.15.cloned.1.call-start = ((), (), s32[]{:S(2)}) async-start(), calls=%async_computation.22 | async-start | bytes 5308416 | tf_op jit(solution)/shard_map/reduce_scatter | solution.py:253
  294.2 1.1 copy-start.3
  310.1 20.2 %all-to-all-start.10 = ((bf16[4,2,49152]{2,1,0:T(2,128)(2,1)}), bf16[4,2,49152]{2,1,0:T(2,128)(2,1)S(1)}, u32[]{:S(2)}, u32[]{:S(2)}) async-start(bf16[4,2,49152]{2,1,0:T(2,128)(2,1)} %reshape.206), calls=%async_computation.15 | async-start | bytes 1572864 | tf_op jit(solution)/shard_map/all_to_all | solution.py:177
  313.6 331.9 %reduce-scatter.17.cloned.1.call-start = ((), (), s32[]{:S(2)}) async-start(), calls=%async_computation.23 | async-start | bytes 5308416 | tf_op jit(solution)/shard_map/reduce_scatter | solution.py:256
  347.7 0.9 copy-start.17
  349.5 8.7 %all-to-all-start.7 = ((bf16[4,64,384]{2,0,1:T(4,128)(2,1)}), bf16[4,64,384]{2,0,1:T(4,128)(2,1)S(1)}, u32[]{:S(2)}, u32[]{:S(2)}) async-start(bf16[4,64,384]{2,0,1:T(4,128)(2,1)} %copy.130), calls=%async_computation.7 | async-start | bytes 393216 | tf_op jit(solution)/shard_map/all_to_all | solution.py:193
  358.2 18.1 %all-to-all-start.5 = ((bf16[4,320,384]{2,0,1:T(4,128)(2,1)}), bf16[4,320,384]{2,0,1:T(4,128)(2,1)}, u32[]{:S(2)}, u32[]{:S(2)}) async-start(bf16[4,320,384]{2,0,1:T(4,128)(2,1)} %copy.121), calls=%async_computation.5 | async-start | bytes 1966080 | tf_op jit(solution)/shard_map/all_to_all | solution.py:194
  376.2 18.3 %all-to-all-start.6 = ((bf16[4,320,384]{2,0,1:T(4,128)(2,1)}), bf16[4,320,384]{2,0,1:T(4,128)(2,1)}, u32[]{:S(2)}, u32[]{:S(2)}) async-start(bf16[4,320,384]{2,0,1:T(4,128)(2,1)} %copy.125), calls=%async_computation.6 | async-start | bytes 1966080 | tf_op jit(solution)/shard_map/all_to_all | solution.py:195
  396.0 9.4 %slice-start = ((s8[4718592]{0:T(1024)(128)(4,1)}), s8[4194304]{0:T(1024)(128)(4,1)S(1)}, s32[]{:S(2)}) async-start(s8[4718592]{0:T(1024)(128)(4,1)} %bitcast.178), calls=%async_computation.24 | async-start | bytes 8388608
  400.3 4.3 copy-start.20
  400.3 4.3 copy-start.25
  400.3 4.3 copy-start.31
  400.3 5.1 slice-start.1
  404.6 3.0 copy-start.7
  404.6 1.2 copy-start.5
  404.6 1.2 copy-start.23
  404.6 1.2 copy-start.29
  404.6 1.2 copy-start.35
  405.8 1.8 copy-start.32
  405.8 1.8 copy-start.33
  405.8 47.2 %copy-start.11 = (f32[4,16,1536]{2,1,0:T(8,128)S(1)}, f32[4,16,1536]{2,1,0:T(8,128)}, u32[]{:S(2)}) copy-start(f32[4,16,1536]{2,1,0:T(8,128)} %get-tuple-element.39) | copy-start | bytes 1179652
  405.8 47.2 %copy-start.15 = (bf16[4,16,1536]{2,1,0:T(8,128)(2,1)S(1)}, bf16[4,16,1536]{2,1,0:T(8,128)(2,1)}, u32[]{:S(2)}) copy-start(bf16[4,16,1536]{2,1,0:T(8,128)(2,1)} %param.31) | copy-start | bytes 589828
  405.8 47.1 %copy-start.22 = (f32[4,16]{1,0:T(4,128)S(1)}, f32[4,16]{1,0:T(4,128)}, u32[]{:S(2)}) copy-start(f32[4,16]{1,0:T(4,128)} %copy-done.21) | copy-start | bytes 772
  405.8 47.1 %copy-start.27 = (f32[4,16]{1,0:T(4,128)S(1)}, f32[4,16]{1,0:T(4,128)}, u32[]{:S(2)}) copy-start(f32[4,16]{1,0:T(4,128)} %copy-done.26) | copy-start | bytes 772
  405.8 47.1 %copy-start.37 = (f32[4,16]{1,0:T(4,128)S(1)}, f32[4,16]{1,0:T(4,128)}, u32[]{:S(2)}) copy-start(f32[4,16]{1,0:T(4,128)} %copy-done.36) | copy-start | bytes 772
  405.8 47.1 %copy-start.39 = (f32[4,16]{1,0:T(4,128)S(1)}, f32[4,16]{1,0:T(4,128)}, u32[]{:S(2)}) copy-start(f32[4,16]{1,0:T(4,128)} %copy-done.38) | copy-start | bytes 772
  405.8 47.1 %copy-start.43 = (f32[4]{0:T(128)S(1)}, f32[4]{0:T(128)}, u32[]{:S(2)}) copy-start(f32[4]{0:T(128)} %copy-done.42) | copy-start | bytes 52
  449.4 4.7 copy-start.8
Sparse Core Ops, SparseCore 0:
  61.1 40.2 all-gather.1
Sparse Core Ops, SparseCore 1:
  184.0 65.9 reduce-scatter.12
  253.2 63.0 reduce-scatter.6
  319.6 63.0 reduce-scatter.8
  386.0 63.1 reduce-scatter.10
  452.9 94.1 reduce-scatter.14
  550.7 94.8 reduce-scatter.16
where the time goes:
time: 667 us; the launch traced here: 656 us
  waiting for transfers between devices  225 us (34%)
  local copies, waits for them, and re-layouts  142 us (21%)
  matrix products  111 us (17%)
  blocking collectives  95.7 us (14%)
  starting transfers between devices  39.3 us (6%)
  other arithmetic  25.7 us (4%)
  between operations  16.9 us (3%)
    reduce_scatter x1, waiting for transfers between devices, body(): lax.psum_scatter(down_part.astype(jnp.bfloat16), 'rows', scatter_dimensio...  96.3 us
    reduce_scatter x1, waiting for transfers between devices, body(): lax.psum_scatter(up_part.astype(jnp.bfloat16), 'rows', scatter_dimension=...  84.6 us
    unnamed x110, local copies, waits for them, and re-layouts  60.4 us
    unnamed x1, blocking collectives  41.8 us
    all_gather x1, blocking collectives, body(): lax.all_gather(d_out, 'head', axis=1, tiled=True)  16.7 us
    all_gather x1, blocking collectives, body(): lax.all_gather(ffn_norm, 'head', axis=1, tiled=True)  16.7 us
    all_to_all x1, waiting for transfers between devices, body(): lax.all_to_all(keys, 'head', split_axis=2, concat_axis=1, tiled=True)  15 us
    dot_general x1, matrix products, body(): jnp.einsum('ilf,df->ild', d_hidden, w_up, preferred_element_type=jnp.floa...  13.6 us
  transfers between devices with their start and end apart: 17, of which 8 were waited for; matrix products, arithmetic and copies ran while one was open for 39% of the time, Pallas kernels for 0%

commit v1 on v0

v1 whole, which is shorter than its diff:
```python
import functools
import math

import jax
import jax.numpy as jnp
from jax import lax
from jax.experimental import pallas as pl
from jax.experimental.pallas import tpu as pltpu
from jax.sharding import PartitionSpec as P

HEAD_DIM = 96
MAX_IMG = 8
EPSILON = 1e-05
BF = jnp.bfloat16
F32 = jnp.float32
MESH = pl.DeviceIdType.MESH
ANY = pl.BlockSpec(memory_space=pl.ANY)


def factor_rows(count):
    nz = 4 if count % 4 == 0 else 1
    return nz, count // nz


def factor_head(count):
    nc = 2 if count % 2 == 0 else 1
    return count // nc, nc


def standardize(values):
    row_mean = jnp.mean(values, axis=-1, keepdims=True)
    centered = values - row_mean
    variance = jnp.mean(centered * centered, axis=-1, keepdims=True)
    inv_scale = lax.rsqrt(variance + EPSILON)
    return centered * inv_scale, inv_scale


def norm_back(d_scaled, normed, inv_scale):
    first_mean = jnp.mean(d_scaled, axis=-1, keepdims=True)
    second_mean = jnp.mean(d_scaled * normed, axis=-1, keepdims=True)
    return inv_scale * (d_scaled - first_mean - normed * second_mean)


def dot(a, b, dims):
    return lax.dot_general(a, b, (dims, ((), ())), preferred_element_type=F32)


class Place:
    def __init__(self, rows, heads):
        self.rows, self.heads = rows, heads
        self.nz, self.nx = factor_rows(rows)
        self.ny, self.nc = factor_head(heads)
        self.r = lax.axis_index("rows")
        self.h = lax.axis_index("head")
        self.z, self.x = self.r // self.nx, self.r % self.nx
        self.y, self.c = self.h // self.nc, self.h % self.nc

    def head_peers(self):
        return [(self.r, lax.rem(self.h + d, self.heads)) for d in range(1, self.heads)]

    def x_peer(self, d):
        return lax.rem(self.x + d, self.nx)

    def z_peer(self, d):
        return lax.rem(self.z + d, self.nz)

    def y_peer(self, d):
        return lax.rem(self.y + d, self.ny)


def greet(peers):
    barrier = pltpu.get_barrier_semaphore()
    for peer in peers:
        pl.semaphore_signal(barrier, inc=1, device_id=peer, device_id_type=MESH)
    pl.semaphore_wait(barrier, len(peers))


def remote(src, dst, sems, slot, peer):
    return pltpu.make_async_remote_copy(
        src_ref=src,
        dst_ref=dst,
        send_sem=sems[0].at[slot],
        recv_sem=sems[1].at[slot],
        device_id=peer,
        device_id_type=MESH,
    )


def run_kernel(kernel, name, ident, out_shapes, semaphores, *operands, scratch=()):
    return pl.pallas_call(
        kernel,
        name=name,
        out_shape=out_shapes,
        in_specs=[ANY] * len(operands),
        out_specs=jax.tree.map(lambda _: ANY, out_shapes),
        scratch_shapes=[pltpu.SemaphoreType.DMA((semaphores,))] * 2
        + [pltpu.SemaphoreType.DMA((len(operands),))]
        + list(scratch),
        compiler_params=pltpu.CompilerParams(collective_id=ident, has_side_effects=True),
    )(*operands)


def gather_head_kernel(rows, heads, count, put_second, *refs):
    ins, outs = refs[:count], refs[count : 2 * count]
    sems, local = refs[2 * count : 2 * count + 2], refs[2 * count + 2]
    at = Place(rows, heads)

    def slot(ref, head):
        return ref.at[:, head] if put_second else ref.at[head]

    greet(at.head_peers())
    partner = (at.r, at.y * at.nc + (at.nc - 1 - at.c))
    own, far, near, relay = [], [], [], []
    per = 2 * at.ny
    for i in range(count):
        for d in range(1, at.ny):
            peer = (at.r, at.y_peer(d) * at.nc + at.c)
            copy = remote(ins[i], slot(outs[i], at.h), sems, i * per + d, peer)
            copy.start()
            far.append((i, d, copy))
        if at.nc > 1:
            copy = remote(ins[i], slot(outs[i], at.h), sems, i * per, partner)
            copy.start()
            near.append(copy)
        copy = pltpu.make_async_copy(ins[i], slot(outs[i], at.h), local.at[i])
        copy.start()
        own.append(copy)
    for i, d, copy in far:
        copy.wait_recv()
        source = at.y_peer(at.ny - d) * at.nc + at.c
        if at.nc > 1:
            block = slot(outs[i], source)
            hop = remote(block, block, sems, i * per + at.ny + d, partner)
            hop.start()
            relay.append(hop)
    for copy in near:
        copy.wait_recv()
    for copy in relay:
        copy.wait_recv()
    for copy in own:
        copy.wait()
    for _, _, copy in far:
        copy.wait_send()
    for copy in near + relay:
        copy.wait_send()


def gather_head(name, ident, rows, heads, put_second, *operands):
    shapes = []
    for array in operands:
        shape = array.shape
        shape = shape[:1] + (heads,) + shape[1:] if put_second else (heads,) + shape
        shapes.append(jax.ShapeDtypeStruct(shape, array.dtype))
    ny, _ = factor_head(heads)
    kernel = functools.partial(gather_head_kernel, rows, heads, len(operands), put_second)
    return run_kernel(kernel, name, ident, shapes, len(operands) * 2 * ny, *operands)


def exchange_kernel(rows, heads, axis, ways, count, *refs):
    ins, outs = refs[:count], refs[count : 2 * count]
    sems = refs[2 * count : 2 * count + 2]
    at = Place(rows, heads)
    peers = []
    for a in ways:
        peers += exchange_peers(at, a)
    greet([peer for peer, _ in peers])
    copies = []
    slot = 0
    for i in range(count):
        for d, (peer, index) in enumerate(exchange_peers(at, axis[i])):
            copy = remote(ins[i].at[index], outs[i].at[d], sems, slot, peer)
            copy.start()
            copies.append(copy)
            slot += 1
    for copy in copies:
        copy.wait()


def exchange_peers(at, axis):
    if axis == "head":
        return [((at.r, lax.rem(at.h + d, at.heads)), lax.rem(at.h + d, at.heads)) for d in range(1, at.heads)]
    if axis == "x":
        return [((at.z * at.nx + at.x_peer(d), at.h), at.x_peer(d)) for d in range(1, at.nx)]
    if axis == "z":
        return [((at.z_peer(d) * at.nx + at.x, at.h), at.z_peer(d)) for d in range(1, at.nz)]
    if axis == "y":
        return [((at.r, at.y_peer(d) * at.nc + at.c), at.y_peer(d)) for d in range(1, at.ny)]
    return [((at.r, at.y * at.nc + (at.nc - 1 - at.c)), at.nc - 1 - at.c)]


def exchange(name, ident, rows, heads, axis, *operands):
    shapes = [jax.ShapeDtypeStruct((a.shape[0] - 1,) + a.shape[1:], a.dtype) for a in operands]
    ways = sorted(set(axis))
    total = sum(a.shape[0] - 1 for a in operands)
    kernel = functools.partial(exchange_kernel, rows, heads, axis, ways, len(operands))
    return run_kernel(kernel, name, ident, shapes, total, *operands)


def attend_kernel(q_ref, k_ref, v_ref, o_ref):
    width = q_ref.shape[-1]
    scale = 1.0 / math.sqrt(HEAD_DIM)
    for n in range(width // HEAD_DIM):
        part = slice(n * HEAD_DIM, (n + 1) * HEAD_DIM)
        q, k, v = q_ref[0, :, part], k_ref[0, :, part], v_ref[0, :, part]
        scores = dot(q, k, ((1,), (1,))) * scale
        top = jnp.max(scores, axis=-1, keepdims=True)
        powers = jnp.exp(scores - top)
        total = jnp.sum(powers, axis=-1, keepdims=True)
        probs = (powers * (1.0 / total)).astype(BF)
        o_ref[0, :, part] = dot(probs, v, ((1,), (0,))).astype(BF)


def attend_back_kernel(q_ref, k_ref, v_ref, d_ref, dq_ref, dk_ref, dv_ref):
    width = q_ref.shape[-1]
    scale = 1.0 / math.sqrt(HEAD_DIM)
    for n in range(width // HEAD_DIM):
        part = slice(n * HEAD_DIM, (n + 1) * HEAD_DIM)
        q, k, v, d = q_ref[0, :, part], k_ref[0, :, part], v_ref[0, :, part], d_ref[0, :, part]
        scores = dot(q, k, ((1,), (1,))) * scale
        top = jnp.max(scores, axis=-1, keepdims=True)
        powers = jnp.exp(scores - top)
        probs = powers * (1.0 / jnp.sum(powers, axis=-1, keepdims=True))
        d_probs = dot(d, v, ((1,), (1,)))
        inner = jnp.sum(probs * d_probs, axis=-1, keepdims=True)
        d_scores = (probs * (d_probs - inner)).astype(BF)
        dq_ref[0, :, part] = (dot(d_scores, k, ((1,), (0,))) * scale).astype(BF)
        dk_ref[0, :, part] = (dot(d_scores, q, ((0,), (0,))) * scale).astype(BF)
        dv_ref[0, :, part] = dot(probs.astype(BF), d, ((0,), (0,))).astype(BF)


def per_image(kernel, name, outs, *operands):
    def spec(array):
        return pl.BlockSpec((1,) + array.shape[1:], lambda i: (i, 0, 0))

    return pl.pallas_call(
        kernel,
        name=name,
        grid=(operands[0].shape[0],),
        in_specs=[spec(a) for a in operands],
        out_specs=[spec(a) for a in outs],
        out_shape=outs,
    )(*operands)


def body(
    media, latents, counts, media_gain, media_shift, latent_gain, latent_shift, w_query, w_key, w_value, w_out,
    ffn_gain, ffn_shift, w_up, w_down, cotangent,
):
    rows, heads = lax.axis_size("rows"), lax.axis_size("head")
    at = Place(rows, heads)
    nz, nx, ny, nc = at.nz, at.nx, at.ny, at.nc
    images, patch, width = media.shape
    lat = latents.shape[1]
    hidden_width = w_up.shape[1]
    cols = width // heads
    mine = hidden_width // heads
    lat_rows = heads * lat
    key_count = heads * (patch + lat)

    media_all, lat_all, cot_all = gather_head("gather_inputs", 1, rows, heads, True, media, latents, cotangent)
    wide_all = lat_all.astype(F32)
    media_hat_all, _ = standardize(media_all.astype(F32))
    latent_hat_all, _ = standardize(wide_all)
    media_norm = (media_hat_all * media_gain + media_shift).astype(BF)
    latent_norm = (latent_hat_all * latent_gain + latent_shift).astype(BF)
    key_rows = jnp.concatenate([media_norm, latent_norm], axis=2).reshape(images * key_count, width)
    latent_rows = latent_norm.reshape(images * lat_rows, width)

    def columns(weight):
        return lax.dynamic_slice_in_dim(weight, at.h * cols, cols, 1)

    query = dot(latent_rows, columns(w_query), ((1,), (0,))).astype(BF).reshape(images, lat_rows, cols)
    keys = dot(key_rows, columns(w_key), ((1,), (0,))).astype(BF).reshape(images, key_count, cols)
    values = dot(key_rows, columns(w_value), ((1,), (0,))).astype(BF).reshape(images, key_count, cols)
    q_shape = jax.ShapeDtypeStruct(query.shape, BF)
    k_shape = jax.ShapeDtypeStruct(keys.shape, BF)
    (mixed_mine,) = per_image(attend_kernel, "attend", [q_shape], query, keys, values)
    (mixed_heads,) = gather_head("gather_mixed", 2, rows, heads, False, mixed_mine.reshape(images * lat_rows, cols))
    mixed = jnp.swapaxes(mixed_heads, 0, 1).reshape(images * lat_rows, width)

    residual = wide_all.reshape(images * lat_rows, width) + dot(mixed, w_out, ((1,), (0,)))
    ffn_hat, ffn_scale = standardize(residual)
    ffn_norm = (ffn_hat * ffn_gain + ffn_shift).astype(BF)
    image_ids = at.r * images + jnp.arange(images, dtype=jnp.int32)
    seq_table = jnp.arange(counts.shape[0], dtype=jnp.int32)
    limit = jnp.sum(jnp.where((image_ids // MAX_IMG)[:, None] == seq_table[None, :], counts[None, :], 0), axis=1)
    live = (image_ids % MAX_IMG) < limit
    d_out = jnp.where(live[:, None, None, None], cot_all, jnp.zeros((), BF)).reshape(images * lat_rows, width)

    def gather_rows(array):
        half = array.reshape(nc, array.shape[0] // nc, width)
        part = lax.dynamic_index_in_dim(half, at.c, 0, keepdims=False)
        line = [part]
        for d in range(1, nz):
            line.append(lax.ppermute(part, "rows", [(z * nx + x, (z + d) % nz * nx + x) for z in range(nz) for x in range(nx)]))
        plane = list(line)
        for d in range(1, nx):
            for block in line:
                plane.append(lax.ppermute(block, "rows", [(z * nx + x, z * nx + (x + d) % nx) for z in range(nz) for x in range(nx)]))
        mine_all = jnp.stack(plane)
        if nc == 1:
            return mine_all.reshape(-1, width)
        other = lax.ppermute(mine_all, "head", [(y * nc + c, y * nc + nc - 1 - c) for y in range(ny) for c in range(nc)])
        first = jnp.where(at.c == 0, mine_all, other)
        second = jnp.where(at.c == 0, other, mine_all)
        return jnp.concatenate([first, second], axis=0).reshape(-1, width)

    d_out_rows = gather_rows(d_out)
    ffn_rows = gather_rows(ffn_norm)
    up_mine = lax.dynamic_slice_in_dim(w_up, at.h * mine, mine, 1)
    down_mine = lax.dynamic_slice_in_dim(w_down, at.h * mine, mine, 0)
    hidden = dot(ffn_norm, up_mine, ((1,), (0,)))
    activated_wide, gelu_pull = jax.vjp(jax.nn.gelu, hidden)
    activated = activated_wide.astype(BF)
    out_part = dot(activated, down_mine, ((1,), (0,)))
    d_hidden = gelu_pull(dot(d_out, down_mine, ((1,), (1,))))[0].astype(BF)
    d_ffn_part = dot(d_hidden, up_mine, ((1,), (1,)))

    def by_core(array):
        return jnp.transpose(array.reshape(images, ny, nc, lat, width), (2, 1, 0, 3, 4))

    d_ffn_core, out_core = by_core(d_ffn_part), by_core(out_part)
    if nc > 1:
        d_ffn_other, out_other = exchange("sum_core", 3, rows, heads, ["core", "core"], d_ffn_core, out_core)
        d_ffn_half = lax.dynamic_index_in_dim(d_ffn_core, at.c, 0, keepdims=False) + d_ffn_other[0]
        out_half = lax.dynamic_index_in_dim(out_core, at.c, 0, keepdims=False) + out_other[0]
    else:
        d_ffn_half, out_half = d_ffn_core[0], out_core[0]
    if ny > 1:
        send = d_ffn_half.astype(BF)
        out_send = out_half.astype(BF)
        copies = jnp.broadcast_to(send[None], (ny,) + send.shape)
        d_ffn_far, out_far = exchange("sum_y", 4, rows, heads, ["y", "y"], copies, out_send)
        d_ffn_half = send.astype(F32) + jnp.sum(d_ffn_far.astype(F32), axis=0)
        out_own = lax.dynamic_index_in_dim(out_half, at.y, 0, keepdims=False) + jnp.sum(out_far.astype(F32), axis=0)
    else:
        out_own = out_half[0]
    if nc > 1:
        pair = jnp.broadcast_to(d_ffn_half[None], (nc,) + d_ffn_half.shape)
        (d_ffn_pair,) = exchange("share_core", 5, rows, heads, ["core"], pair)
        first = jnp.where(at.c == 0, d_ffn_half, d_ffn_pair[0])
        second = jnp.where(at.c == 0, d_ffn_pair[0], d_ffn_half)
        both = jnp.stack([first, second])
    else:
        both = d_ffn_half[None]
    d_ffn_norm = jnp.transpose(both, (2, 1, 0, 3, 4)).reshape(images * lat_rows, width)

    def own_rows(array):
        return lax.dynamic_index_in_dim(array.reshape(images, heads, lat, width), at.h, 1, keepdims=False)

    output = own_rows(residual) + jnp.swapaxes(out_own, 0, 0).reshape(images, lat, width)
    d_ffn_own = own_rows(d_ffn_norm)
    ffn_gain_part = jnp.sum(d_ffn_own * own_rows(ffn_hat), axis=(0, 1))
    ffn_shift_part = jnp.sum(d_ffn_own, axis=(0, 1))
    d_residual = d_out.astype(F32) + norm_back(d_ffn_norm * ffn_gain, ffn_hat, ffn_scale)
    d_attn = d_residual.astype(BF)
    out_rows = lax.dynamic_slice_in_dim(w_out, at.h * cols, cols, 0)
    d_mixed = dot(d_attn, out_rows, ((1,), (1,))).astype(BF).reshape(images, lat_rows, cols)
    d_query, d_keys, d_values = per_image(
        attend_back_kernel, "attend_back", [q_shape, k_shape, k_shape], query, keys, values, d_mixed
    )

    d_attn_cols = lax.dynamic_slice_in_dim(d_attn, at.h * cols, cols, 1)
    parts = [
        dot(latent_rows, d_query.reshape(-1, cols), ((0,), (0,))),
        dot(key_rows, d_keys.reshape(-1, cols), ((0,), (0,))),
        dot(key_rows, d_values.reshape(-1, cols), ((0,), (0,))),
        dot(mixed, d_attn_cols, ((0,), (0,))),
    ]
    block = width // rows
    parts = [jnp.swapaxes(p.astype(BF).reshape(nz, nx, block, cols), 0, 1) for p in parts]

    def to_heads(array, count):
        return jnp.swapaxes(array.reshape(images, heads, count, cols), 0, 1)

    turned = [to_heads(d_query, lat), to_heads(d_keys, patch + lat), to_heads(d_values, patch + lat)]
    moved = exchange("turn_and_sum_x", 6, rows, heads, ["head"] * 3 + ["x"] * 4, *turned, *parts)
    full = []
    for array, far in zip(turned, moved[:3]):
        own = lax.dynamic_index_in_dim(array, at.h, 0, keepdims=True)
        stacked = jnp.concatenate([own, far], axis=0)
        stacked = jnp.take(stacked, (at.h - jnp.arange(heads)) % heads, axis=0)
        full.append(jnp.transpose(stacked, (1, 2, 0, 3)).reshape(-1, width))
    d_query_own, d_keys_own, d_values_own = full
    sums = [
        (lax.dynamic_index_in_dim(p, at.x, 0, keepdims=False).astype(F32) + jnp.sum(far.astype(F32), axis=0)).astype(BF)
        for p, far in zip(parts, moved[3:])
    ]

    d_key_rows = (dot(d_keys_own, w_key, ((1,), (1,))) + dot(d_values_own, w_value, ((1,), (1,)))).reshape(
        images, patch + lat, width
    )
    d_media_norm = d_key_rows[:, :patch]
    d_latent_norm = d_key_rows[:, patch:] + dot(d_query_own, w_query, ((1,), (1,))).reshape(images, lat, width)
    media_hat, media_scale = standardize(media.astype(F32))
    latent_hat, latent_scale = standardize(latents.astype(F32))
    media_grad = norm_back(d_media_norm * media_gain, media_hat, media_scale)
    latents_grad = own_rows(d_residual) + norm_back(d_latent_norm * latent_gain, latent_hat, latent_scale)
    vectors = jnp.stack(
        [
            jnp.sum(d_media_norm * media_hat, axis=(0, 1)),
            jnp.sum(d_media_norm, axis=(0, 1)),
            jnp.sum(d_latent_norm * latent_hat, axis=(0, 1)),
            jnp.sum(d_latent_norm, axis=(0, 1)),
            ffn_gain_part,
            ffn_shift_part,
        ]
    )
    share = width // (rows * heads)
    tiles = jnp.transpose(vectors.reshape(6, rows, heads, share), (2, 1, 0, 3))
    tiles = jnp.pad(tiles, ((0, 0), (0, 0), (0, 2), (0, 128 - share)))
    moved = exchange("sum_z", 7, rows, heads, ["z"] * 4 + ["head"], *sums, tiles)
    grads = [
        lax.dynamic_index_in_dim(s, at.z, 0, keepdims=False).astype(F32) + jnp.sum(far.astype(F32), axis=0)
        for s, far in zip(sums, moved[:4])
    ]
    tiles = lax.dynamic_index_in_dim(tiles, at.h, 0, keepdims=False) + jnp.sum(moved[4], axis=0)
    tiles = tiles.reshape(nz, nx, 8, 128)
    (far,) = exchange("vectors_z", 8, rows, heads, ["z"], tiles)
    tiles = lax.dynamic_index_in_dim(tiles, at.z, 0, keepdims=False) + jnp.sum(far, axis=0)
    if nx > 1:
        (far,) = exchange("vectors_x", 9, rows, heads, ["x"], tiles)
        tiles = lax.dynamic_index_in_dim(tiles, at.x, 0, keepdims=False) + jnp.sum(far, axis=0)
    else:
        tiles = tiles[0]
    vector_sums = tiles[:6, :share]

    hidden_rows = dot(ffn_rows, up_mine, ((1,), (0,)))
    activated_rows, gelu_pull = jax.vjp(jax.nn.gelu, hidden_rows)
    d_hidden_rows = gelu_pull(dot(d_out_rows, down_mine, ((1,), (1,))))[0].astype(BF)
    ffn_cols = lax.dynamic_slice_in_dim(ffn_rows, at.r * block, block, 1)
    d_out_cols = lax.dynamic_slice_in_dim(d_out_rows, at.r * block, block, 1)
    up_grad = dot(ffn_cols, d_hidden_rows, ((0,), (0,)))
    down_grad = dot(activated_rows.astype(BF), d_out_cols, ((0,), (0,)))
    return (
        output, media_grad, latents_grad, vector_sums[0], vector_sums[1], vector_sums[2], vector_sums[3],
        grads[0], grads[1], grads[2], grads[3], vector_sums[4], vector_sums[5], up_grad, down_grad,
    )


def solution(mesh):
    row = P("rows", "head", None)
    whole = P()
    vector = P(("rows", "head"))
    grid = P("rows", "head")
    return jax.shard_map(
        body,
        mesh=mesh,
        in_specs=(row, row) + (whole,) * 13 + (row,),
        out_specs=(row, row, row, vector, vector, vector, vector, grid, grid, grid, grid, vector, vector, grid, P("head", "rows")),
        check_vma=False,
    )
```

time: 667 us -> 506 us (0.76)
  Pallas kernels: 0 us -> 211 us
  waiting for transfers between devices: 225 us -> 41.5 us
  blocking collectives: 95.7 us -> 0 us
  local copies, waits for them, and re-layouts: 142 us -> 51.2 us
  other arithmetic: 25.7 us -> 68.4 us
  starting transfers between devices: 39.3 us -> 16.6 us
  between operations: 16.9 us -> 2.24 us
    pallas_call x0 -> x11, Pallas kernels: none -> 211 us  [the longest x9 191 us: run_kernel(): pl.pallas_call(kernel, name=name, out_shape=out_shapes, in_specs=[ANY] *...]
    reduce_scatter x6 -> x0, waiting for transfers between devices: 181 us -> none  [the longest x1 96.3 us: body(): lax.psum_scatter(down_part.astype(jnp.bfloat16), 'rows', scatter_dimensio...]
    unnamed x110 -> x148, local copies, waits for them, and re-layouts: 60.4 us -> 14.8 us
    all_to_all x10 -> x0, waiting for transfers between devices: 44.3 us -> none  [the longest x1 15 us: body(): lax.all_to_all(keys, 'head', split_axis=2, concat_axis=1, tiled=True)]
    all_gather x3 -> x0, blocking collectives: 44.3 us -> none  [the longest x1 16.7 us: body(): lax.all_gather(d_out, 'head', axis=1, tiled=True)]
    unnamed x1 -> x0, blocking collectives: 41.8 us -> none
    ppermute x0 -> x16, waiting for transfers between devices: none -> 41.5 us  [the longest x8 26.1 us: gather_rows(): lax.ppermute(block, 'rows', [(z * nx + x, z * nx + (x + d) % nx) for z in...]
    all_to_all x10 -> x0, starting transfers between devices: 39 us -> none  [the longest x1 4.5 us: body(): lax.all_to_all(d_triple[2], 'head', split_axis=1, concat_axis=2, tiled=True)]
  transfers between devices with their start and end apart: 17 -> 16, of which waited for: 8 -> 3; matrix products, arithmetic and copies ran while one was open for 39% -> 31% of each run, Pallas kernels for 0% -> 31%
where the time goes in v1:
time: 506 us; the launch traced here: 497 us
  Pallas kernels  211 us (42%)
  matrix products  106 us (21%)
  other arithmetic  68.4 us (14%)
  local copies, waits for them, and re-layouts  51.2 us (10%)
  waiting for transfers between devices  41.5 us (8%)
  starting transfers between devices  16.6 us (3%)
    pallas_call x9, Pallas kernels, run_kernel(): pl.pallas_call(kernel, name=name, out_shape=out_shapes, in_specs=[ANY] *...  191 us
    dot_general x18, matrix products, dot(): return lax.dot_general(a, b, (dims, ((), ())), preferred_element_type=F32)  106 us
    ppermute x8, waiting for transfers between devices, gather_rows(): lax.ppermute(block, 'rows', [(z * nx + x, z * nx + (x + d) % nx) for z in...  26.1 us
    pallas_call x2, Pallas kernels, per_image(): pl.pallas_call(kernel, name=name, grid=(operands[0].shape[0],), in_specs=...  20.6 us
    ppermute x6, waiting for transfers between devices, gather_rows(): lax.ppermute(part, 'rows', [(z * nx + x, (z + d) % nz * nx + x) for z in...  15.4 us
    unnamed x148, local copies, waits for them, and re-layouts  14.8 us
  transfers between devices with their start and end apart: 16, of which 3 were waited for; matrix products, arithmetic and copies ran while one was open for 31% of the time, Pallas kernels for 31%

profile of v1, /device:TPU:0, one launch (start us, length us, event | category | flops | bytes accessed | tf_op | source)
XLA Modules:
  0.0 497.2 jit_solution(9084893924056772528)
XLA Ops:
  0.7 40.1 %gather_inputs.1 = (bf16[4,4,64,1536]{3,2,1,0:T(8,128)(2,1)}, bf16[4,4,16,1536]{3,2,1,0:T(8,128)(2,1)}, bf16[4,4,16,1536]{3,2,1,0:T(8,128)(2,1)}) custom-call(bf16[4,64,1536]{2,1,0:T(8,128)(2,1)} %refs_0_.1, bf16[4,16,1536]{2,1,0:T(8,128)(2,1)} %refs_1_.1, bf16[4,16,1536]{2,1,0:T(8,128)(2,1)} %refs_2_.1), custom_call_target="tpu_custom_call" | custom-call | tf_op jit(solution)/shard_map/gather_inputs/pallas_call | solution.py:90
  40.8 2.5 convert_reduce_fusion
  47.4 5.4 %convolution_convert_fusion.2 = bf16[1280,384]{1,0:T(8,128)(2,1)} fusion(bf16[1280,1536]{1,0:T(8,128)(2,1)S(1)} %bitcast.259, bf16[1536,1536]{1,0:T(8,128)(2,1)} %param.27, s32[]{:T(128)S(6)} %select_n.186), kind=kOutput, calls=%fused_computation.47 | convolution fusion | flops 1510440960 | bytes 6094852 | tf_op jit(solution)/shard_map/dot_general | solution.py:45
  52.8 4.4 convolution_convert_fusion.3
  57.2 2.6 fusion.67
  59.8 8.2 %attend.1 = bf16[4,64,384]{2,1,0:T(8,128)(2,1)} custom-call(bf16[4,64,384]{2,1,0:T(8,128)(2,1)} %bitcast.288, bf16[4,320,384]{2,1,0:T(8,128)(2,1)} %bitcast.257, bf16[4,320,384]{2,1,0:T(8,128)(2,1)} %bitcast.255), custom_call_target="tpu_custom_call" | custom-call | tf_op jit(solution)/shard_map/attend/pallas_call | solution.py:235
  68.0 9.0 %gather_mixed.1 = bf16[4,256,384]{2,1,0:T(8,128)(2,1)} custom-call(bf16[256,384]{1,0:T(8,128)(2,1)} %bitcast.290), custom_call_target="tpu_custom_call" | custom-call | tf_op jit(solution)/shard_map/gather_mixed/pallas_call | solution.py:90
  78.5 3.8 fusion.149
  83.3 1.5 add_convert_fusion
  86.6 1.5 collective-permute-start.3
  88.1 3.6 collective-permute-start.2
  99.8 4.0 fusion.32
  103.8 5.6 %fusion.22 = f32[256,1536]{1,0:T(8,128)} fusion(bf16[6144,1536]{1,0:T(8,128)(2,1)} %param.32, s32[]{:T(128)S(6)} %select_n.188, f32[256,1536]{1,0:T(8,128)S(1)} %fusion.32), kind=kOutput, calls=%fused_computation.32 | convolution fusion | flops 1211498496 | bytes 7864324 | tf_op jit(solution)/shard_map/dot_general | solution.py:45
  109.4 8.8 %fusion.30 = f32[256,1536]{1,0:T(8,128)} fusion(bf16[1536,6144]{1,0:T(8,128)(2,1)} %param.31, s32[]{:T(128)S(6)} %select_n.188, f32[256,1536]{1,0:T(8,128)} %copy-done.64, bf16[256,1536]{1,0:T(8,128)(2,1)} %bitcast.252, bf16[6144,1536]{1,0:T(8,128)(2,1)} %param.32), kind=kOutput, calls=%fused_computation.36 | convolution fusion | flops 2423783424 | bytes 13370368 | tf_op jit(solution)/shard_map/dot_general | solution.py:45
  118.2 2.9 copy.169
  122.4 3.8 sum_core.1
  126.2 1.5 fusion.77
  127.7 2.5 convert_bitcast_fusion
  131.1 15.7 %sum_y.1 = (bf16[1,2,4,16,1536]{4,3,2,1,0:T(8,128)(2,1)}, bf16[1,4,16,1536]{3,2,1,0:T(8,128)(2,1)}) custom-call(bf16[2,2,4,16,1536]{4,3,2,1,0:T(8,128)(2,1)} %broadcast_in_dim.56.refs_0_, bf16[2,4,16,1536]{3,2,1,0:T(8,128)(2,1)} %get-tuple-element.72.refs_1_), custom_call_target="tpu_custom_call" | custom-call | tf_op jit(solution)/shard_map/sum_y/pallas_call | solution.py:90
  148.0 1.4 broadcast_in_dim.58.refs_0_
  149.4 2.7 share_core.1
  152.0 1.4 fusion.89
  155.2 2.3 multiply_reduce_fusion
  158.1 3.0 fusion.142
  161.1 2.5 fusion.70
  163.6 1.6 convolution_convert_fusion.4
  165.2 12.4 %attend_back.1 = (bf16[4,64,384]{2,1,0:T(8,128)(2,1)}, bf16[4,320,384]{2,1,0:T(8,128)(2,1)}, bf16[4,320,384]{2,1,0:T(8,128)(2,1)}) custom-call(bf16[4,64,384]{2,1,0:T(8,128)(2,1)} %bitcast.289, bf16[4,320,384]{2,1,0:T(8,128)(2,1)} %bitcast.258, bf16[4,320,384]{2,1,0:T(8,128)(2,1)} %bitcast.256, bf16[4,64,384]{2,1,0:T(8,128)(2,1)} %bitcast.292), custom_call_target="tpu_custom_call" | custom-call | tf_op jit(solution)/shard_map/attend_back/pallas_call | solution.py:235
  177.7 1.7 copy.167
  180.8 1.7 dynamic-slice_bitcast_fusion.3
  182.5 2.3 copy.166
  184.8 1.7 dynamic-slice_bitcast_fusion.2
  191.9 2.6 copy.170
  196.3 2.2 convolution_convert_fusion
  198.5 2.2 convolution_convert_fusion.1
  203.0 54.1 %turn_and_sum_x.1 = (bf16[3,4,16,384]{3,2,1,0:T(8,128)(2,1)}, bf16[3,4,80,384]{3,2,1,0:T(8,128)(2,1)}, bf16[3,4,80,384]{3,2,1,0:T(8,128)(2,1)}, bf16[1,4,192,384...) custom-call(bf16[4,4,16,384]{3,2,1,0:T(8,128)(2,1)} %bitcast.291, ...), custom_call_target="tpu_custom_call" | custom-call | tf_op jit(solution)/shard_map/turn_and_sum_x/pallas_call | solution.py:90
  257.2 2.2 fusion.57.refs_3_
  259.4 2.2 fusion.58.refs_2_
  265.6 1.6 gather_fusion.1
  268.5 1.6 gather_fusion.2
  270.2 1.8 select_bitcast_fusion
  273.8 4.4 fusion.150
  278.3 1.7 convolution_add_fusion
  283.7 4.7 fusion.100
  290.7 53.5 %sum_z.1 = (bf16[3,192,384]{2,1,0:T(8,128)(2,1)}, bf16[3,192,384]{2,1,0:T(8,128)(2,1)}, bf16[3,192,384]{2,1,0:T(8,128)(2,1)}, bf16[3,192,384]{2,1,0:T(8,128)(2,1)}, f32[3,8,8,128]{3,2,1,0:T(8,128)}) custom-call(bf16[4,192,384]{2,1,0:T(8,128)(2,1)} %fusion.60.refs_0_, bf16[4,192,384]{2,1,0:T(8,128)(2,1)} %fusion.59.refs_1_, ...), custom_call_target="tpu_custom_call" | custom-call | tf_op jit(solution)/shard_map/sum_z/pallas_call | solution.py:90
  345.8 7.7 %vectors_z.1 = f32[3,2,8,128]{3,2,1,0:T(8,128)} custom-call(f32[4,2,8,128]{3,2,1,0:T(8,128)} %add.355.refs_0_), custom_call_target="tpu_custom_call" | custom-call | tf_op jit(solution)/shard_map/vectors_z/pallas_call | solution.py:90
  355.6 3.9 vectors_x.1
  361.9 1.7 convert_add_fusion.8
  364.7 1.7 convert_add_fusion.7
  366.4 1.7 convert_add_fusion.6
  368.1 1.7 convert_add_fusion.5
  369.9 3.2 fusion.44
  373.2 2.0 fusion.99
  376.0 3.3 collective-permute-start.10
  385.2 8.2 %collective-permute-done.4 = bf16[128,1536]{1,0:T(8,128)(2,1)S(1)} collective-permute-done((bf16[128,1536]{1,0:T(8,128)(2,1)}, bf16[128,1536]{1,0:T(8,128)(2,1)S(1)}, u32[]{:S(2)}, u32[]{:S(2)}) %collective-permute-start.4) | collective-permute-done | bytes 393248 | tf_op jit(solution)/shard_map/ppermute | solution.py:299
  394.1 1.5 collective-permute-start.6
  395.5 15.4 %collective-permute-done.9 = bf16[128,1536]{1,0:T(8,128)(2,1)S(1)} collective-permute-done((bf16[128,1536]{1,0:T(8,128)(2,1)}, bf16[128,1536]{1,0:T(8,128)(2,1)S(1)}, u32[]{:S(2)}, u32[]{:S(2)}) %collective-permute-start.9) | collective-permute-done | bytes 393248 | tf_op jit(solution)/shard_map/ppermute | solution.py:295
  411.4 1.6 collective-permute-start.13
  415.9 1.8 bitcast_dynamic-update-slice_fusion.3
  417.7 17.8 %collective-permute-done.12 = bf16[128,1536]{1,0:T(8,128)(2,1)S(1)} collective-permute-done((bf16[128,1536]{1,0:T(8,128)(2,1)S(1)}, bf16[128,1536]{1,0:T(8,128)(2,1)S(1)}, u32[]{:S(2)}, u32[]{:S(2)}) %collective-permute-start.12) | collective-permute-done | bytes 393248 | tf_op jit(solution)/shard_map/ppermute | solution.py:299
  438.8 16.7 %fusion.28 = f32[2048,1536]{1,0:T(8,128)} fusion(bf16[2048,1536]{1,0:T(8,128)(2,1)S(1)} %bitcast.246, bf16[1536,6144]{1,0:T(8,128)(2,1)} %param.31, s32[]{:T(128)S(6)} %select_n.188), kind=kOutput, calls=%fused_computation.34 | convolution fusion | flops 9663676416 | bytes 23592964 | tf_op jit(solution)/shard_map/dot_general | solution.py:45
  455.5 3.3 broadcast_select_fusion.1
  458.8 3.2 pad_maximum_fusion.1
  461.9 25.8 %fusion.14 = f32[192,1536]{1,0:T(8,128)} fusion(f32[2048,1536]{1,0:T(8,128)} %fusion.28, bf16[2048,1536]{1,0:T(8,128)(2,1)} %bitcast.248, bf16[6144,1536]{1,0:T(8,128)(2,1)} %param.32, s32[]{:T(128)S(6)} %select_n.188, bf16[2048,1536]{1,0:T(8,128)(2,1)} %bitcast.247, s32[]{:T(128)S(6)} %select_n.213), kind=kOutput, calls=%fused_computation.24 | convolution fusion | flops 10934550528 | bytes 25821192 | tf_op jit(solution)/shard_map/dot_general | solution.py:45
  487.7 9.0 %fusion.13 = f32[1536,192]{0,1:T(8,128)} fusion(f32[2048,1536]{1,0:T(8,128)} %fusion.28, bf16[2048,1536]{1,0:T(8,128)(2,1)} %bitcast.249, s32[]{:T(128)S(6)} %select_n.213), kind=kOutput, calls=%fused_computation.23 | convolution fusion | flops 1236271104 | bytes 14811140 | tf_op jit(solution)/shard_map/dot_general | solution.py:45
  (266 shorter events, 66.8 us)
Async XLA Ops:
  40.8 3.8 copy-start.4
  47.0 10.2 %copy-start.10 = (bf16[4,4,16,1536]{3,2,1,0:T(8,128)(2,1)}, bf16[4,4,16,1536]{3,2,1,0:T(8,128)(2,1)S(1)}, u32[]{:S(2)}) copy-start(bf16[4,4,16,1536]{3,2,1,0:T(8,128)(2,1)S(1)} %add_convert_fusion.1) | copy-start | bytes 2359300
  47.4 5.4 %copy-start.19 = (bf16[4,4,80,1536]{3,2,1,0:T(8,128)(2,1)}, bf16[4,4,80,1536]{3,2,1,0:T(8,128)(2,1)S(1)}, u32[]{:S(2)}) copy-start(bf16[4,4,80,1536]{3,2,1,0:T(8,128)(2,1)S(1)} %pad_maximum_fusion.2) | copy-start | bytes 11796484
  57.2 21.3 %copy-start.6 = (bf16[4,4,16,1536]{3,2,1,0:T(8,128)(2,1)S(1)}, bf16[4,4,16,1536]{3,2,1,0:T(8,128)(2,1)}, u32[]{:S(2)}) copy-start(bf16[4,4,16,1536]{3,2,1,0:T(8,128)(2,1)} %get-tuple-element.38) | copy-start | bytes 2359300
  78.5 4.8 copy-start.36
  78.5 4.7 copy-start.54
  82.3 11.1 %copy-start.63 = (s32[4]{0:T(128)S(1)}, s32[4]{0:T(128)}, u32[]{:S(2)}) copy-start(s32[4]{0:T(128)} %param.20) | copy-start | bytes 52
  83.2 15.1 %copy-start.1 = (bf16[4,64,1536]{2,1,0:T(8,128)(2,1)S(1)}, bf16[4,64,1536]{2,1,0:T(8,128)(2,1)}, u32[]{:S(2)}) copy-start(bf16[4,64,1536]{2,1,0:T(8,128)(2,1)} %refs_0_.1) | copy-start | bytes 2359300
  84.8 14.4 %copy-start.15 = (bf16[4,16,1536]{2,1,0:T(8,128)(2,1)S(1)}, bf16[4,16,1536]{2,1,0:T(8,128)(2,1)}, u32[]{:S(2)}) copy-start(bf16[4,16,1536]{2,1,0:T(8,128)(2,1)} %refs_1_.1) | copy-start | bytes 589828
  86.6 296.9 %collective-permute-start.3 = (bf16[128,1536]{1,0:T(8,128)(2,1)}, bf16[128,1536]{1,0:T(8,128)(2,1)}, u32[]{:S(2)}, u32[]{:S(2)}) collective-permute-start(bf16[128,1536]{1,0:T(8,128)(2,1)} %get-tuple-element.96), channel_id=1, source_target_pairs={{0,4},{4,0},{8,12},{12,8},{16,20},{20,16},{24,28},{28,24},{1,5},{5... | collective-permute-start | bytes 1179656 | tf_op jit(solution)/shard_map/ppermute | solution.py:299
  88.1 293.3 %collective-permute-start.2 = (bf16[128,1536]{1,0:T(8,128)(2,1)}, bf16[128,1536]{1,0:T(8,128)(2,1)}, u32[]{:S(2)}, u32[]{:S(2)}) collective-permute-start(bf16[128,1536]{1,0:T(8,128)(2,1)} %get-tuple-element.96), channel_id=1, source_target_pairs={{0,24},{4,28},{8,0},{12,4},{16,8},{20,12},{24,16},{28,20},{1,25},{... | collective-permute-start | bytes 1179656 | tf_op jit(solution)/shard_map/ppermute | solution.py:295
  91.7 288.6 %collective-permute-start.1 = (bf16[128,1536]{1,0:T(8,128)(2,1)}, bf16[128,1536]{1,0:T(8,128)(2,1)}, u32[]{:S(2)}, u32[]{:S(2)}) collective-permute-start(bf16[128,1536]{1,0:T(8,128)(2,1)} %get-tuple-element.96), channel_id=1, source_target_pairs={{0,16},{4,20},{8,24},{12,28},{16,0},{20,4},{24,8},{28,12},{1,17},{... | collective-permute-start | bytes 1179656 | tf_op jit(solution)/shard_map/ppermute | solution.py:295
  91.7 284.2 %collective-permute-start = (bf16[128,1536]{1,0:T(8,128)(2,1)}, bf16[128,1536]{1,0:T(8,128)(2,1)}, u32[]{:S(2)}, u32[]{:S(2)}) collective-permute-start(bf16[128,1536]{1,0:T(8,128)(2,1)} %get-tuple-element.96), channel_id=1, source_target_pairs={{0,8},{4,12},{8,16},{12,20},{16,24},{20,28},{24,0},{28,4},{1,9},{5... | collective-permute-start | bytes 1179656 | tf_op jit(solution)/shard_map/ppermute | solution.py:295
  96.8 319.1 %collective-permute-start.11 = (bf16[128,1536]{1,0:T(8,128)(2,1)}, bf16[128,1536]{1,0:T(8,128)(2,1)}, u32[]{:S(2)}, u32[]{:S(2)}) collective-permute-start(bf16[128,1536]{1,0:T(8,128)(2,1)} %get-tuple-element.94), channel_id=1, source_target_pairs={{0,4},{4,0},{8,12},{12,8},{16,20},{20,16},{24,28},{28,24},{1,5},{5... | collective-permute-start | bytes 1179656 | tf_op jit(solution)/shard_map/ppermute | solution.py:299
  103.8 5.6 %copy-start.64 = (f32[256,1536]{1,0:T(8,128)}, f32[256,1536]{1,0:T(8,128)S(1)}, u32[]{:S(2)}) copy-start(f32[256,1536]{1,0:T(8,128)S(1)} %fusion.32) | copy-start | bytes 4718596
  153.8 3.7 copy-start.51
  177.6 8.8 %copy-start.26 = (bf16[4,320,384]{2,1,0:T(8,128)(2,1)S(1)}, bf16[4,320,384]{2,1,0:T(8,128)(2,1)}, u32[]{:S(2)}) copy-start(bf16[4,320,384]{2,1,0:T(8,128)(2,1)} %get-tuple-element.47) | copy-start | bytes 2949124
  177.7 9.8 %copy-start.58 = (f32[4,64]{1,0:T(4,128)S(1)}, f32[4,64]{1,0:T(4,128)}, u32[]{:S(2)}) copy-start(f32[4,64]{1,0:T(4,128)} %convert_reduce_fusion.1) | copy-start | bytes 3076
  177.7 10.8 %copy-start.55 = (f32[4,16]{1,0:T(4,128)S(1)}, f32[4,16]{1,0:T(4,128)}, u32[]{:S(2)}) copy-start(f32[4,16]{1,0:T(4,128)} %convert_reduce_fusion.7) | copy-start | bytes 772
  177.7 10.8 %copy-start.16 = (bf16[4,16,1536]{2,1,0:T(8,128)(2,1)S(1)}, bf16[4,16,1536]{2,1,0:T(8,128)(2,1)}, u32[]{:S(2)}) copy-start(bf16[4,16,1536]{2,1,0:T(8,128)(2,1)} %refs_1_.1) | copy-start | bytes 589828
  177.7 11.6 %copy-start.61 = (s32[4]{0:T(128)S(1)}, s32[4]{0:T(128)}, u32[]{:S(2)}) copy-start(s32[4]{0:T(128)} %get-tuple-element.109) | copy-start | bytes 52
  177.7 11.6 %copy-start.62 = (s32[4]{0:T(128)S(1)}, s32[4]{0:T(128)}, u32[]{:S(2)}) copy-start(s32[4]{0:T(128)} %fusion.121) | copy-start | bytes 52
  186.4 8.1 %copy-start.11 = (bf16[4,4,16,1536]{3,2,1,0:T(8,128)(2,1)S(1)}, bf16[4,4,16,1536]{3,2,1,0:T(8,128)(2,1)}, u32[]{:S(2)}) copy-start(bf16[4,4,16,1536]{3,2,1,0:T(8,128)(2,1)} %copy-done.10) | copy-start | bytes 2359300
  186.4 8.1 %copy-start.28 = (bf16[4,64,384]{2,1,0:T(8,128)(2,1)S(1)}, bf16[4,64,384]{2,1,0:T(8,128)(2,1)}, u32[]{:S(2)}) copy-start(bf16[4,64,384]{2,1,0:T(8,128)(2,1)} %get-tuple-element.46) | copy-start | bytes 589828
  191.9 4.3 copy-start.20
  191.9 4.3 copy-start.27
  203.0 54.2 %copy-start.8 = (bf16[4,2,192,384]{3,2,0,1:T(8,128)(2,1)S(1)}, bf16[4,2,192,384]{3,2,0,1:T(8,128)(2,1)}, u32[]{:S(2)}) copy-start(bf16[4,2,192,384]{3,2,0,1:T(8,128)(2,1)} %copy.170) | copy-start | bytes 3538948
  257.1 4.5 copy-start.9
  257.1 4.5 copy-start.30
  257.2 5.4 %copy-start.7 = (bf16[4,2,192,384]{3,2,0,1:T(8,128)(2,1)S(1)}, bf16[4,2,192,384]{3,2,0,1:T(8,128)(2,1)}, u32[]{:S(2)}) copy-start(bf16[4,2,192,384]{3,2,0,1:T(8,128)(2,1)} %copy.173) | copy-start | bytes 3538948
  257.2 5.4 %copy-start.29 = (bf16[1,4,192,384]{3,2,1,0:T(8,128)(2,1)S(1)}, bf16[1,4,192,384]{3,2,1,0:T(8,128)(2,1)}, u32[]{:S(2)}) copy-start(bf16[1,4,192,384]{3,2,1,0:T(8,128)(2,1)} %get-tuple-element.51) | copy-start | bytes 1769476
  257.2 6.4 %copy-start.34 = (bf16[1,4,16,384]{3,2,1,0:T(8,128)(2,1)S(1)}, bf16[1,4,16,384]{3,2,1,0:T(8,128)(2,1)}, u32[]{:S(2)}) copy-start(bf16[1,4,16,384]{3,2,1,0:T(8,128)(2,1)} %dynamic-slice_bitcast_fusion.4) | copy-start | bytes 147460
  257.2 6.4 %copy-start.35 = (bf16[3,4,16,384]{3,2,1,0:T(8,128)(2,1)S(1)}, bf16[3,4,16,384]{3,2,1,0:T(8,128)(2,1)}, u32[]{:S(2)}) copy-start(bf16[3,4,16,384]{3,2,1,0:T(8,128)(2,1)} %get-tuple-element.50) | copy-start | bytes 442372
  259.4 4.8 copy-start.59
  265.6 4.6 copy-start.60
  272.9 5.3 %slice-start = ((s8[4718592]{0:T(1024)(128)(4,1)}), s8[4194304]{0:T(1024)(128)(4,1)S(1)}, s32[]{:S(2)}) async-start(s8[4718592]{0:T(1024)(128)(4,1)} %bitcast.295), calls=%async_computation | async-start | bytes 8388608
  273.8 4.4 slice-start.1
  278.3 5.4 %copy-start.17 = (bf16[4,16,1536]{2,1,0:T(8,128)(2,1)S(1)}, bf16[4,16,1536]{2,1,0:T(8,128)(2,1)}, u32[]{:S(2)}) copy-start(bf16[4,16,1536]{2,1,0:T(8,128)(2,1)} %refs_1_.1) | copy-start | bytes 589828
  278.3 5.4 %copy-start.39 = (f32[1536]{0:T(1024)S(1)}, f32[1536]{0:T(1024)}, u32[]{:S(2)}) copy-start(f32[1536]{0:T(1024)} %param.23) | copy-start | bytes 18436
  278.3 5.4 %copy-start.45 = (f32[4,16]{1,0:T(4,128)S(1)}, f32[4,16]{1,0:T(4,128)}, u32[]{:S(2)}) copy-start(f32[4,16]{1,0:T(4,128)} %copy-done.44) | copy-start | bytes 772
  278.3 5.4 %copy-start.48 = (f32[4,16]{1,0:T(4,128)S(1)}, f32[4,16]{1,0:T(4,128)}, u32[]{:S(2)}) copy-start(f32[4,16]{1,0:T(4,128)} %add_rsqrt_fusion.2) | copy-start | bytes 772
  283.7 6.1 %copy-start.40 = (f32[1,8,4,48]{3,0,1,2:T(1,128)S(1)}, f32[1,8,4,48]{3,0,1,2:T(1,128)}, u32[]{:S(2)}) copy-start(f32[1,8,4,48]{3,0,1,2:T(1,128)} %copy.141) | copy-start | bytes 18436
  283.7 6.1 %copy-start.41 = (f32[1,8,4,48]{3,0,1,2:T(1,128)S(1)}, f32[1,8,4,48]{3,0,1,2:T(1,128)}, u32[]{:S(2)}) copy-start(f32[1,8,4,48]{3,0,1,2:T(1,128)} %copy.140) | copy-start | bytes 18436
  344.2 22.2 %copy-start.32 = (bf16[3,192,384]{2,1,0:T(8,128)(2,1)S(1)}, bf16[3,192,384]{2,1,0:T(8,128)(2,1)}, u32[]{:S(2)}) copy-start(bf16[3,192,384]{2,1,0:T(8,128)(2,1)} %get-tuple-element.58) | copy-start | bytes 1327108
  344.2 23.9 %copy-start.31 = (bf16[3,192,384]{2,1,0:T(8,128)(2,1)S(1)}, bf16[3,192,384]{2,1,0:T(8,128)(2,1)}, u32[]{:S(2)}) copy-start(bf16[3,192,384]{2,1,0:T(8,128)(2,1)} %get-tuple-element.59) | copy-start | bytes 1327108
  368.1 7.0 %copy-start.22 = (f32[1,2,4,16,1536]{4,3,2,1,0:T(8,128)S(1)}, f32[1,2,4,16,1536]{4,3,2,1,0:T(8,128)}, u32[]{:S(2)}) copy-start(f32[1,2,4,16,1536]{4,3,2,1,0:T(8,128)} %get-tuple-element.73) | copy-start | bytes 2359300
  368.1 7.0 %copy-start.33 = (bf16[1,4,16,1536]{3,2,1,0:T(8,128)(2,1)S(1)}, bf16[1,4,16,1536]{3,2,1,0:T(8,128)(2,1)}, u32[]{:S(2)}) copy-start(bf16[1,4,16,1536]{3,2,1,0:T(8,128)(2,1)} %get-tuple-element.43) | copy-start | bytes 589828
  369.9 3.3 copy-start.46
  369.9 3.3 copy-start.49
  369.9 3.3 copy-start.56
  369.9 3.3 copy-start.57
  369.9 9.4 %copy-start.18 = (bf16[8,128,1536]{2,1,0:T(8,128)(2,1)S(1)}, bf16[8,128,1536]{2,1,0:T(8,128)(2,1)}, u32[]{:S(2)}) copy-start(bf16[8,128,1536]{2,1,0:T(8,128)(2,1)} %get-tuple-element.97) | copy-start | bytes 9437188
  376.0 18.1 %collective-permute-start.10 = (bf16[128,1536]{1,0:T(8,128)(2,1)}, bf16[128,1536]{1,0:T(8,128)(2,1)S(1)}, u32[]{:S(2)}, u32[]{:S(2)}) collective-permute-start(bf16[128,1536]{1,0:T(8,128)(2,1)} %get-tuple-element.94), channel_id=1, source_target_pairs={{0,24},{4,28},{8,0},{12,4},{16,8},{20,12},{24,16},{28,20},{1,25},{... | collective-permute-start | bytes 1179656 | tf_op jit(solution)/shard_map/ppermute | solution.py:295
  380.3 30.6 %collective-permute-start.9 = (bf16[128,1536]{1,0:T(8,128)(2,1)}, bf16[128,1536]{1,0:T(8,128)(2,1)S(1)}, u32[]{:S(2)}, u32[]{:S(2)}) collective-permute-start(bf16[128,1536]{1,0:T(8,128)(2,1)} %get-tuple-element.94), channel_id=1, source_target_pairs={{0,16},{4,20},{8,24},{12,28},{16,0},{20,4},{24,8},{28,12},{1,17},{... | collective-permute-start | bytes 1179656 | tf_op jit(solution)/shard_map/ppermute | solution.py:295
  381.5 29.9 %collective-permute-start.8 = (bf16[128,1536]{1,0:T(8,128)(2,1)}, bf16[128,1536]{1,0:T(8,128)(2,1)S(1)}, u32[]{:S(2)}, u32[]{:S(2)}) collective-permute-start(bf16[128,1536]{1,0:T(8,128)(2,1)} %get-tuple-element.94), channel_id=1, source_target_pairs={{0,8},{4,12},{8,16},{12,20},{16,24},{20,28},{24,0},{28,4},{1,9},{5... | collective-permute-start | bytes 1179656 | tf_op jit(solution)/shard_map/ppermute | solution.py:295
  383.6 9.8 %collective-permute-start.4 = (bf16[128,1536]{1,0:T(8,128)(2,1)}, bf16[128,1536]{1,0:T(8,128)(2,1)S(1)}, u32[]{:S(2)}, u32[]{:S(2)}) collective-permute-start(bf16[128,1536]{1,0:T(8,128)(2,1)} %collective-permute-done), channel_id=1, source_target_pairs={{0,4},{4,0},{8,12},{12,8},{16,20},{20,16},{24,28},{28,24},{1,5},{5... | collective-permute-start | bytes 1179656 | tf_op jit(solution)/shard_map/ppermute | solution.py:299
  393.4 19.5 %collective-permute-start.5 = (bf16[128,1536]{1,0:T(8,128)(2,1)}, bf16[128,1536]{1,0:T(8,128)(2,1)S(1)}, u32[]{:S(2)}, u32[]{:S(2)}) collective-permute-start(bf16[128,1536]{1,0:T(8,128)(2,1)} %collective-permute-done.1), channel_id=1, source_target_pairs={{0,4},{4,0},{8,12},{12,8},{16,20},{20,16},{24,28},{28,24},{1,5},{5... | collective-permute-start | bytes 1179656 | tf_op jit(solution)/shard_map/ppermute | solution.py:299
  394.1 19.4 %collective-permute-start.6 = (bf16[128,1536]{1,0:T(8,128)(2,1)}, bf16[128,1536]{1,0:T(8,128)(2,1)S(1)}, u32[]{:S(2)}, u32[]{:S(2)}) collective-permute-start(bf16[128,1536]{1,0:T(8,128)(2,1)} %collective-permute-done.2), channel_id=1, source_target_pairs={{0,4},{4,0},{8,12},{12,8},{16,20},{20,16},{24,28},{28,24},{1,5},{5... | collective-permute-start | bytes 1179656 | tf_op jit(solution)/shard_map/ppermute | solution.py:299
  410.9 26.2 %collective-permute-start.14 = (bf16[128,1536]{1,0:T(8,128)(2,1)S(1)}, bf16[128,1536]{1,0:T(8,128)(2,1)S(1)}, u32[]{:S(2)}, u32[]{:S(2)}) collective-permute-start(bf16[128,1536]{1,0:T(8,128)(2,1)S(1)} %collective-permute-done.10), channel_id=1, source_target_pairs={{0,4},{4,0},{8,12},{12,8},{16,20},{20,16},{24,28},{28,24},{1,5},{5... | collective-permute-start | bytes 1179656 | tf_op jit(solution)/shard_map/ppermute | solution.py:299
  411.4 24.9 %collective-permute-start.13 = (bf16[128,1536]{1,0:T(8,128)(2,1)S(1)}, bf16[128,1536]{1,0:T(8,128)(2,1)S(1)}, u32[]{:S(2)}, u32[]{:S(2)}) collective-permute-start(bf16[128,1536]{1,0:T(8,128)(2,1)S(1)} %collective-permute-done.9), channel_id=1, source_target_pairs={{0,4},{4,0},{8,12},{12,8},{16,20},{20,16},{24,28},{28,24},{1,5},{5... | collective-permute-start | bytes 1179656 | tf_op jit(solution)/shard_map/ppermute | solution.py:299
  412.9 22.5 %collective-permute-start.12 = (bf16[128,1536]{1,0:T(8,128)(2,1)S(1)}, bf16[128,1536]{1,0:T(8,128)(2,1)S(1)}, u32[]{:S(2)}, u32[]{:S(2)}) collective-permute-start(bf16[128,1536]{1,0:T(8,128)(2,1)S(1)} %collective-permute-done.8), channel_id=1, source_target_pairs={{0,4},{4,0},{8,12},{12,8},{16,20},{20,16},{24,28},{28,24},{1,5},{5... | collective-permute-start | bytes 1179656 | tf_op jit(solution)/shard_map/ppermute | solution.py:299
  413.5 24.4 %collective-permute-start.7 = (bf16[8,128,1536]{2,1,0:T(8,128)(2,1)S(1)}, bf16[8,128,1536]{2,1,0:T(8,128)(2,1)S(1)}, u32[]{:S(2)}, u32[]{:S(2)}) collective-permute-start(bf16[8,128,1536]{2,1,0:T(8,128)(2,1)S(1)} %bitcast_dynamic-update-slice_fusion.7), channel_id=1, source_target_pairs={{0,1},{1,0},{2,3},{3,2},{4,5},{5,4},{6,7},{7,6},{8,9},{9,8},{10,11... | collective-permute-start | bytes 9437192 | tf_op jit(solution)/shard_map/ppermute | solution.py:303
  437.8 17.7 %collective-permute-start.15 = (bf16[8,128,1536]{2,1,0:T(8,128)(2,1)}, bf16[8,128,1536]{2,1,0:T(8,128)(2,1)}, u32[]{:S(2)}, u32[]{:S(2)}) collective-permute-start(bf16[8,128,1536]{2,1,0:T(8,128)(2,1)} %bitcast_dynamic-update-slice_fusion), channel_id=1, source_target_pairs={{0,1},{1,0},{2,3},{3,2},{4,5},{5,4},{6,7},{7,6},{8,9},{9,8},{10,11... | collective-permute-start | bytes 9437192 | tf_op jit(solution)/shard_map/ppermute | solution.py:303
  438.8 16.7 %copy-start.13 = (bf16[16,128,1536]{2,1,0:T(8,128)(2,1)}, bf16[16,128,1536]{2,1,0:T(8,128)(2,1)S(1)}, u32[]{:S(2)}) copy-start(bf16[16,128,1536]{2,1,0:T(8,128)(2,1)S(1)} %pad_maximum_fusion) | copy-start | bytes 18874372
  (19 other events, 39.2 us)

commit v2 on v1

v2 whole, which is shorter than its diff:
```python
import functools
import math
import types

import jax
import jax.numpy as jnp
from jax import lax
from jax.experimental import pallas as pl
from jax.experimental.pallas import tpu as pltpu
from jax.sharding import PartitionSpec as P

HEAD_DIM = 96
MAX_IMG = 8
EPSILON = 1e-05
BF = jnp.bfloat16
F32 = jnp.float32
MESH = pl.DeviceIdType.MESH
ANY = pl.BlockSpec(memory_space=pl.ANY)


def factor_rows(count):
    nz = 4 if count % 4 == 0 else 1
    return nz, count // nz


def factor_head(count):
    nc = 2 if count % 2 == 0 else 1
    return count // nc, nc


def standardize(values):
    row_mean = jnp.mean(values, axis=-1, keepdims=True)
    centered = values - row_mean
    variance = jnp.mean(centered * centered, axis=-1, keepdims=True)
    inv_scale = lax.rsqrt(variance + EPSILON)
    return centered * inv_scale, inv_scale


def norm_back(d_scaled, normed, inv_scale):
    first_mean = jnp.mean(d_scaled, axis=-1, keepdims=True)
    second_mean = jnp.mean(d_scaled * normed, axis=-1, keepdims=True)
    return inv_scale * (d_scaled - first_mean - normed * second_mean)


def dot(a, b, dims):
    return lax.dot_general(a, b, (dims, ((), ())), preferred_element_type=F32)


class Place:
    def __init__(self, rows, heads):
        self.rows, self.heads = rows, heads
        self.nz, self.nx = factor_rows(rows)
        self.ny, self.nc = factor_head(heads)
        self.r = lax.axis_index("rows")
        self.h = lax.axis_index("head")
        self.z, self.x = self.r // self.nx, self.r % self.nx
        self.y, self.c = self.h // self.nc, self.h % self.nc

    def head_peers(self):
        return [(self.r, lax.rem(self.h + d, self.heads)) for d in range(1, self.heads)]

    def x_peer(self, d):
        return lax.rem(self.x + d, self.nx)

    def z_peer(self, d):
        return lax.rem(self.z + d, self.nz)

    def y_peer(self, d):
        return lax.rem(self.y + d, self.ny)


def greet(peers):
    barrier = pltpu.get_barrier_semaphore()
    for peer in peers:
        pl.semaphore_signal(barrier, inc=1, device_id=peer, device_id_type=MESH)
    pl.semaphore_wait(barrier, len(peers))


def remote(src, dst, sems, slot, peer):
    return pltpu.make_async_remote_copy(
        src_ref=src,
        dst_ref=dst,
        send_sem=sems[0].at[slot],
        recv_sem=sems[1].at[slot],
        device_id=peer,
        device_id_type=MESH,
    )


class Copies:
    def __init__(self, at, send, recv):
        self.at, self.send, self.recv, self.used = at, send, recv, 0
        self.unsent = []

    def put(self, src, dst, peer):
        copy = pltpu.make_async_remote_copy(
            src_ref=src,
            dst_ref=dst,
            send_sem=self.send.at[self.used],
            recv_sem=self.recv.at[self.used],
            device_id=peer,
            device_id_type=MESH,
        )
        self.used += 1
        copy.start()
        self.unsent.append(copy)
        return copy

    def sent(self, copy):
        copy.wait_send()
        self.unsent = [c for c in self.unsent if c is not copy]

    def finish(self):
        for copy in self.unsent:
            copy.wait_send()


def norm_rows(block):
    mean = jnp.mean(block, axis=-1, keepdims=True)
    centered = block - mean
    scale = lax.rsqrt(jnp.mean(centered * centered, axis=-1, keepdims=True) + EPSILON)
    return centered * scale, scale


def mm(a, b):
    return dot(a, b, ((1,), (0,)))


def mt(a, b):
    return dot(a, b, ((1,), (1,)))


def tm(a, b):
    return dot(a, b, ((0,), (0,)))


def gelu_pair(v):
    c = math.sqrt(2.0 / math.pi)
    square = v * v
    t = jnp.tanh(c * v * (1.0 + 0.044715 * square))
    half = 0.5 * (1.0 + t)
    slope = half + 0.5 * v * (1.0 - t * t) * (c * (1.0 + 3.0 * 0.044715 * square))
    return v * half, slope


def loop(count, step):
    def run(i, carry):
        step(i)
        return carry

    lax.fori_loop(0, count, run, 0)


def tile_of(extent, most):
    size = most
    while extent % size:
        size -= 128
    return size


def forward_kernel(s, *refs):
    refs = dict(zip(s.names, refs, strict=True))
    n = types.SimpleNamespace(**refs)
    at = Place(s.rows, s.heads)
    ny, nc, nz, nx = at.ny, at.nc, at.nz, at.nx
    G, pl_rows, ll, D, E, F = s.images, s.patch, s.lat, s.width, s.cols, s.mine
    M, L, LR = G * pl_rows, G * ll, s.heads * ll
    GL = G * LR
    copies = Copies(at, n.send, n.recv)
    partner = (at.r, at.y * nc + (nc - 1 - at.c))
    loads = []

    def load(src, dst):
        copy = pltpu.make_async_copy(src, dst, n.local.at[len(loads)])
        copy.start()
        loads.append(copy)
        return copy

    load_cot = load(n.cot, n.cot_v)
    load_media = load(n.media, n.raw_m.at[0])
    load_lat = load(n.lat, n.raw_l.at[0])

    def columns(weight):
        if weight.shape[1] == E:
            return weight
        return weight.at[:, pl.ds(pl.multiple_of(at.h * E, 128), E)]

    load_qkv = [load(columns(w), v) for w, v in ((n.wk, n.wk_v), (n.wv, n.wv_v), (n.wq, n.wq_v))]

    greet(at.head_peers() + [(at.z * nx + at.x_peer(d), at.h) for d in range(1, nx)] + [(at.z_peer(d) * nx + at.x, at.h) for d in range(1, nz)])
    load_cot.wait()
    masked = n.cot_v[...].astype(F32) * n.mask[...]
    n.dslot[at.y, at.c] = masked.astype(BF)

    def y_send(src, dst):
        return [copies.put(src, dst(d), (at.r, at.y_peer(d) * nc + at.c)) for d in range(1, ny)]

    def slot(ref):
        return lambda d: ref.at[(ny - d) % ny * nc]

    cot_far = y_send(n.dslot.at[at.y, at.c], lambda d: n.dslot.at[at.y, at.c])
    lat_far = y_send(n.lat, slot(n.raw_l))
    media_far = y_send(n.media, slot(n.raw_m))
    near = []
    if nc > 1:
        lat_near = copies.put(n.lat, n.raw_l.at[1], partner)
        media_near = copies.put(n.media, n.raw_m.at[1], partner)
        cot_near = copies.put(n.dslot.at[at.y, at.c], n.dslot.at[at.y, at.c], partner)
    here = at.r

    def z_send(src, dst):
        return [copies.put(src, dst, (at.z_peer(d) * nx + at.x, at.h)) for d in range(1, nz)]

    def x_send(src, dst):
        return [copies.put(src, dst, (at.z * nx + at.x_peer(d), at.h)) for d in range(1, nx)]

    def quarter(ref, r, d):
        return ref.at[r, pl.ds(pl.multiple_of((at.c * ny + at.y_peer(d)) * L, 16), L)]

    own = n.dslot.at[at.y, at.c]
    z_far = {0: z_send(own, quarter(n.dall, here, 0))}
    x_far = x_send(own, quarter(n.dall, here, 0))
    load_out = load(n.wout, n.wout_v)
    load_up = load(n.wup.at[:, pl.ds(pl.multiple_of(at.h * F, 128), F)], n.wup_v)
    load_down = load(n.wdown.at[pl.ds(pl.multiple_of(at.h * F, 16), F)], n.wdown_v)

    def x_forward(d):
        for dz, copy in enumerate(z_far[d], 1):
            copy.wait_recv()
            block = quarter(n.dall, at.z_peer(nz - dz) * nx + at.x, d)
            x_far.extend(x_send(block, block))

    stores, kept = [], [0]

    def store(src, dst):
        copy = pltpu.make_async_copy(src, dst, n.out_sem.at[kept[0]])
        kept[0] += 1
        copy.start()
        stores.append(copy)
        return copy

    busy = {}

    def patches(k, place):
        buf = place % 2
        if buf in busy:
            busy[buf].wait()
            stores[:] = [c for c in stores if c is not busy[buf]]

        def step(i):
            rows = pl.ds(pl.multiple_of(i * 32, 32), 32)
            hat, _ = norm_rows(n.raw_m[k, rows].astype(F32))
            n.norm[buf, rows] = (hat * n.vecs[0:1] + n.vecs[1:2]).astype(BF)

        loop(M // 32, step)
        n.keys[k] = mm(n.norm[buf], n.wk_v[...]).astype(BF)
        n.values[k] = mm(n.norm[buf], n.wv_v[...]).astype(BF)
        busy[buf] = store(n.norm.at[buf], n.key_norm_o.at[k, 0:M])

    load_media.wait()
    for copy in load_qkv:
        copy.wait()
    patches(0, 0)
    order = 1
    if nc > 1:
        media_near.wait_recv()
        patches(1, order)
        order += 1
    relays = []
    cot_relay, lat_relay, media_relay = [], [], []
    for d, copy in zip(range(1, ny), cot_far):
        copy.wait_recv()
        y = at.y_peer(ny - d)
        if nc > 1:
            cot_relay.append(copies.put(n.dslot.at[y, at.c], n.dslot.at[y, at.c], partner))
    for d, copy in zip(range(1, ny), lat_far):
        copy.wait_recv()
        k = (ny - d) * nc
        if nc > 1:
            lat_relay.append(copies.put(n.raw_l.at[k], n.raw_l.at[k + 1], partner))
    load_lat.wait()
    if nc > 1:
        lat_near.wait_recv()
    for copy in lat_relay:
        copy.wait_recv()
    for d in range(ny):
        for e in range(nc):
            head = at.y_peer(d) * nc + (at.c if e == 0 else nc - 1 - at.c)
            wide = n.raw_l[d * nc + e].astype(F32)
            for i in range(G):
                n.resid[pl.ds(pl.multiple_of(i * LR + head * ll, 8), ll)] = wide[i * ll : (i + 1) * ll]

    for k in range(s.heads):

        def latent_step(i):
            rows = pl.ds(pl.multiple_of(i * 32, 32), 32)
            hat, _ = norm_rows(n.raw_l[k, rows].astype(F32))
            n.lnorm[pl.ds(pl.multiple_of(k * L + i * 32, 32), 32)] = (hat * n.vecs[2:3] + n.vecs[3:4]).astype(BF)

        loop(L // 32, latent_step)
        store(n.lnorm.at[k * L : (k + 1) * L], n.key_norm_o.at[k, M : M + L])
    for weight, result in ((n.wq_v, n.query), (n.wk_v, n.lkeys), (n.wv_v, n.lvalues)):
        wide = mm(n.lnorm[...], weight[...])
        for d in range(ny):
            for e in range(nc):
                head = at.y_peer(d) * nc + (at.c if e == 0 else nc - 1 - at.c)
                for i in range(G):
                    base = (d * nc + e) * L + i * ll
                    n.turn[pl.ds(pl.multiple_of(i * LR + head * ll, 8), ll)] = wide[base : base + ll]
        result[...] = n.turn[...].astype(BF)
    for copy in [load_out, load_up, load_down]:
        copy.wait()
    if nc > 1:
        cot_near.wait_recv()
    for copy in cot_relay:
        copy.wait_recv()
    for y in range(ny):
        for c in range(nc):
            wide = n.dslot[y, c].astype(F32)
            for i in range(G):
                n.part[pl.ds(i * LR + (y * nc + c) * ll, ll)] = wide[i * ll : (i + 1) * ll]
    n.dout[...] = n.part[...].astype(BF)
    store(n.dout, n.dout_o)
    for d in range(1, ny):
        block = n.dslot.at[at.y_peer(d), at.c]
        z_far[d] = z_send(block, quarter(n.dall, here, d))
        x_far.extend(x_send(block, quarter(n.dall, here, d)))
    for d, copy in zip(range(1, ny), media_far):
        copy.wait_recv()
        k = (ny - d) * nc
        if nc > 1:
            media_relay.append(copies.put(n.raw_m.at[k], n.raw_m.at[k + 1], partner))
        patches(k, order)
        order += 1
    for d, copy in zip(range(1, ny), media_relay):
        copy.wait_recv()
        patches((ny - d) * nc + 1, order)
        order += 1
    x_forward(0)
    store(n.keys, n.keys_o)
    store(n.values, n.values_o)
    store(n.lkeys, n.lkeys_o)
    store(n.lvalues, n.lvalues_o)
    store(n.query, n.query_o)

    scale = 1.0 / math.sqrt(HEAD_DIM)

    def attend_image(i):
        q_rows = pl.ds(pl.multiple_of(i * LR, 16), LR)
        m_rows = pl.ds(pl.multiple_of(i * pl_rows, 16), pl_rows)
        q_all = n.query[q_rows]
        k_all = jnp.concatenate([n.keys[k, m_rows] for k in range(s.heads)] + [n.lkeys[q_rows]], axis=0)
        v_all = jnp.concatenate([n.values[k, m_rows] for k in range(s.heads)] + [n.lvalues[q_rows]], axis=0)
        mixed = []
        for j in range(E // HEAD_DIM):
            part = slice(j * HEAD_DIM, (j + 1) * HEAD_DIM)
            scores = mt(q_all[:, part], k_all[:, part]) * scale
            powers = jnp.exp(scores - jnp.max(scores, axis=-1, keepdims=True))
            probs = (powers * (1.0 / jnp.sum(powers, axis=-1, keepdims=True))).astype(BF)
            mixed.append(mm(probs, v_all[:, part]))
        n.mix[at.h, q_rows] = jnp.concatenate(mixed, axis=-1).astype(BF)

    loop(G, attend_image)
    mix_far = y_send(n.mix.at[at.h], lambda d: n.mix.at[at.h])
    mix_near = [copies.put(n.mix.at[at.h], n.mix.at[at.h], partner)] if nc > 1 else []
    wide_tile = tile_of(D, 512)

    def add_mixed(head):
        w_rows = pl.ds(pl.multiple_of(head * E, 16), E)

        def step(t):
            lanes = pl.ds(pl.multiple_of(t * wide_tile, 128), wide_tile)
            n.resid[:, lanes] += mm(n.mix[head], n.wout_v[w_rows, lanes])

        loop(D // wide_tile, step)

    add_mixed(at.h)
    for copy in mix_near:
        copy.wait_recv()
        add_mixed(at.y * nc + (nc - 1 - at.c))
    mix_relay = []
    for d, copy in zip(range(1, ny), mix_far):
        copy.wait_recv()
        y = at.y_peer(ny - d)
        block = n.mix.at[y * nc + at.c]
        if nc > 1:
            mix_relay.append((y, copies.put(block, block, partner)))
        add_mixed(y * nc + at.c)
    for y, copy in mix_relay:
        copy.wait_recv()
        add_mixed(y * nc + (nc - 1 - at.c))
    store(n.mix, n.mixed_o)

    def ffn_step(i):
        rows = pl.ds(pl.multiple_of(i * 32, 32), 32)
        hat, inv = norm_rows(n.resid[rows])
        n.hat[rows] = hat
        n.inv[rows] = jnp.broadcast_to(inv, (32, 128))
        n.ffn[rows] = (hat * n.vecs[4:5] + n.vecs[5:6]).astype(BF)

    loop(GL // 32, ffn_step)
    store(n.ffn, n.ffn_o)

    def own_rows(i):
        return pl.ds(pl.multiple_of(i * LR + at.h * ll, 8), ll)

    quarter_rows = jnp.concatenate([n.hat[own_rows(i)] for i in range(G)], axis=0)
    n.fq[...] = (quarter_rows * n.vecs[4:5] + n.vecs[5:6]).astype(BF)
    ffn_far = z_send(n.fq, quarter(n.fall, here, 0))
    store(n.fq, quarter(n.fall, here, 0))
    hid_tile = 256

    def hidden_step(t):
        lanes = pl.ds(pl.multiple_of(t * hid_tile, 128), hid_tile)
        value, slope = gelu_pair(mm(n.ffn[...], n.wup_v[:, lanes]))
        n.act[:, lanes] = value.astype(BF)
        n.dhid[:, lanes] = (mt(n.dout[...], n.wdown_v[lanes, :]) * slope).astype(BF)

    loop(F // hid_tile, hidden_step)
    store(n.act, n.act_o)
    store(n.dhid, n.dhid_o)

    def back_step(t):
        lanes = pl.ds(pl.multiple_of(t * wide_tile, 128), wide_tile)
        n.part[:, lanes] = mt(n.dhid[...], n.wup_v[lanes, :])

    loop(D // wide_tile, back_step)
    half = GL // nc
    mine_half = pl.ds(pl.multiple_of(at.c * half, 16), half)
    other_half = pl.ds(pl.multiple_of((nc - 1 - at.c) * half, 16), half)
    if nc > 1:
        swap = copies.put(n.part.at[other_half], n.c_recv, partner)

    def out_step(t):
        lanes = pl.ds(pl.multiple_of(t * wide_tile, 128), wide_tile)
        tile = mm(n.act[...], n.wdown_v[:, lanes])
        for i in range(G):
            for head in range(s.heads):
                base = i * LR + head * ll
                n.outp[head % nc, head // nc, i * ll : (i + 1) * ll, lanes] = tile[base : base + ll]

    loop(D // wide_tile, out_step)
    if nc > 1:
        out_swap = copies.put(n.outp.at[nc - 1 - at.c], n.oc_recv, partner)
        swap.wait_recv()
    chunk = 64

    def rows_of(base, i):
        return pl.ds(pl.multiple_of(base + i * chunk, 8), chunk)

    def half_step(i):
        rows = rows_of(at.c * half, i)
        total = n.part[rows]
        if nc > 1:
            total = total + n.c_recv[rows_of(0, i)]
        n.y_send[rows_of(0, i)] = total.astype(BF)

    loop(half // chunk, half_step)
    sum_far = [copies.put(n.y_send, n.y_recv.at[d - 1], (at.r, at.y_peer(d) * nc + at.c)) for d in range(1, ny)]
    if nc > 1:
        out_swap.wait_recv()
    for y in range(ny):
        total = n.outp[at.c, y]
        if nc > 1:
            total = total + n.oc_recv[y]
        n.outp[at.c, y] = total
        n.oy_send[y] = total.astype(BF)
    out_far = [
        copies.put(n.oy_send.at[at.y_peer(d)], n.oy_recv.at[d - 1], (at.r, at.y_peer(d) * nc + at.c)) for d in range(1, ny)
    ]
    for d in range(1, ny):
        x_forward(d)
    for copy in sum_far:
        copy.wait_recv()

    def total_step(i):
        rows = rows_of(0, i)
        total = n.y_send[rows].astype(F32)
        for d in range(1, ny):
            total = total + n.y_recv[d - 1, rows].astype(F32)
        n.share[rows] = total

    loop(half // chunk, total_step)
    if nc > 1:
        share = copies.put(n.share, n.s_recv, partner)

    def residual_back(ref, base):
        def step(i):
            rows = pl.ds(pl.multiple_of(base + i * 32, 8), 32)
            grad = ref[pl.ds(pl.multiple_of(i * 32, 8), 32)]
            hat, inv = n.hat[rows], n.inv[rows, 0:1]
            n.part[rows] = grad
            scaled = grad * n.vecs[4:5]
            first = jnp.mean(scaled, axis=-1, keepdims=True)
            second = jnp.mean(scaled * hat, axis=-1, keepdims=True)
            d_res = n.dout[rows].astype(F32) + inv * (scaled - first - hat * second)
            n.resid[rows] = d_res
            n.dattn[rows] = d_res.astype(BF)

        loop(half // 32, step)

    if nc > 1:
        copies.sent(swap)
    for copy in out_far:
        copy.wait_recv()
    total = n.outp[at.c, at.y]
    for d in range(1, ny):
        total = total + n.oy_recv[d - 1].astype(F32)
    n.own[0] = total + jnp.concatenate([n.resid[own_rows(i)] for i in range(G)], axis=0)
    store(n.own.at[0], n.out_o)
    residual_back(n.share, at.c * half)
    if nc > 1:
        share.wait_recv()
        residual_back(n.s_recv, (nc - 1 - at.c) * half)
    store(n.dattn, n.dattn_o)
    n.own[1] = jnp.concatenate([n.resid[own_rows(i)] for i in range(G)], axis=0)
    store(n.own.at[1], n.dres_o)
    grad = jnp.concatenate([n.part[own_rows(i)] for i in range(G)], axis=0)
    n.fvec[...] = jnp.concatenate(
        [
            jnp.sum(grad * jnp.concatenate([n.hat[own_rows(i)] for i in range(G)], axis=0), axis=0, keepdims=True),
            jnp.sum(grad, axis=0, keepdims=True),
            jnp.zeros((6, D), F32),
        ],
        axis=0,
    )
    store(n.fvec, n.fvec_o)
    for copy in x_far:
        copy.wait_recv()
    if nc > 1:
        spread = []
        for r in range(1, s.rows):
            block = n.dall.at[lax.rem(here + r, s.rows), pl.ds(pl.multiple_of(at.c * ny * L, 16), ny * L)]
            spread.append(copies.put(block, block, partner))
        for copy in spread:
            copy.wait_recv()
    for copy in ffn_far:
        copy.wait_recv()
    copies.finish()
    for copy in stores:
        copy.wait()


def forward(s, media, lat, cot, mask, vecs, wq, wk, wv, wout, wup, wdown):
    ny, nc = factor_head(s.heads)
    G, L, D, E, F = s.images, s.images * s.lat, s.width, s.cols, s.mine
    M, GL, H = s.images * s.patch, s.images * s.lat * s.heads, s.heads
    half = GL // nc
    outs = dict(
        out_o=((L, D), F32), dres_o=((L, D), F32), fvec_o=((8, D), F32), key_norm_o=((H, M + L, D), BF), keys_o=((H, M, E), BF), values_o=((H, M, E), BF), lkeys_o=((GL, E), BF),
        lvalues_o=((GL, E), BF), query_o=((GL, E), BF), mixed_o=((H, GL, E), BF), dattn_o=((GL, D), BF),
        ffn_o=((GL, D), BF), dout_o=((GL, D), BF), act_o=((GL, F), BF), dhid_o=((GL, F), BF),
        dall=((s.rows, GL, D), BF), fall=((s.rows, GL, D), BF),
    )
    scratch = dict(
        cot_v=((L, D), BF), raw_m=((H, M, D), BF), raw_l=((H, L, D), BF), dslot=((ny, nc, L, D), BF),
        norm=((2, M, D), BF), lnorm=((GL, D), BF), turn=((GL, E), F32), keys=((H, M, E), BF), values=((H, M, E), BF), lkeys=((GL, E), BF),
        lvalues=((GL, E), BF), query=((GL, E), BF), mix=((H, GL, E), BF), resid=((GL, D), F32), hat=((GL, D), F32),
        inv=((GL, 128), F32), ffn=((GL, D), BF), dout=((GL, D), BF), act=((GL, F), BF), dhid=((GL, F), BF),
        part=((GL, D), F32), outp=((nc, ny, L, D), F32), c_recv=((half, D), F32), oc_recv=((ny, L, D), F32),
        y_send=((half, D), BF), y_recv=((max(ny - 1, 1), half, D), BF), oy_send=((ny, L, D), BF),
        oy_recv=((max(ny - 1, 1), L, D), BF), share=((half, D), F32), s_recv=((half, D), F32), fq=((L, D), BF),
        own=((2, L, D), F32), dattn=((GL, D), BF), fvec=((8, D), F32),
        wq_v=((D, E), BF), wk_v=((D, E), BF), wv_v=((D, E), BF), wout_v=((D, D), BF), wup_v=((D, F), BF), wdown_v=((F, D), BF),
    )
    ins = dict(media=media, lat=lat, cot=cot, mask=mask, vecs=vecs, wq=wq, wk=wk, wv=wv, wout=wout, wup=wup, wdown=wdown)
    vmem = pl.BlockSpec(memory_space=pltpu.VMEM)
    s.names = list(ins) + list(outs) + list(scratch) + ["send", "recv", "local", "out_sem"]
    result = pl.pallas_call(
        functools.partial(forward_kernel, s),
        name="forward",
        out_shape=[jax.ShapeDtypeStruct(*o) for o in outs.values()],
        in_specs=[vmem if k in ("mask", "vecs") else ANY for k in ins],
        out_specs=[ANY] * len(outs),
        scratch_shapes=[pltpu.VMEM(*v) for v in scratch.values()]
        + [pltpu.SemaphoreType.DMA((200,)), pltpu.SemaphoreType.DMA((200,)), pltpu.SemaphoreType.DMA((16,)), pltpu.SemaphoreType.DMA((40,))],
        compiler_params=pltpu.CompilerParams(collective_id=1, has_side_effects=True, vmem_limit_bytes=60 << 20),
        cost_estimate=pl.CostEstimate(flops=8 * 10**9, bytes_accessed=4 * 10**7, transcendentals=10**6),
    )(*ins.values())
    return dict(zip(outs, result, strict=True))


def window_of(position, block, width):
    base = jnp.minimum(position * block // 128 * 128, width - 256)
    return pl.multiple_of(base, 128), position * block - base


def backward_kernel(s, *refs):
    n = types.SimpleNamespace(**dict(zip(s.names, refs, strict=True)))
    at = Place(s.rows, s.heads)
    ny, nc, nz, nx, H = at.ny, at.nc, at.nz, at.nx, s.heads
    G, pl_rows, ll, D, E, F = s.images, s.patch, s.lat, s.width, s.cols, s.mine
    M, L, LR = G * pl_rows, G * ll, H * ll
    GL, ML, B = G * LR, M + L, s.width // s.rows
    here = at.r
    copies = Copies(at, n.send, n.recv)
    other = nc - 1 - at.c
    partner = (at.r, at.y * nc + other)
    count = [0]

    def load(src, dst):
        copy = pltpu.make_async_copy(src, dst, n.local.at[count[0]])
        count[0] += 1
        copy.start()
        return copy

    def head_of(k):
        d, e = divmod(k, nc)
        return at.y_peer(d) * nc + (at.c if e == 0 else other)

    def quarter(r, y):
        return r, pl.ds(pl.multiple_of((at.c * ny + y) * L, 16), L)

    def group(dz, dx):
        return lax.rem(at.z + dz, nz) * nx + lax.rem(at.x + dx, nx)

    aligned = E % 128 == 0
    first_loads = [load(n.dattn, n.dattn_v), load(n.mixed, n.mix_v)]
    head_lanes = pl.ds(pl.multiple_of(at.h * E, 128), E) if aligned else None
    first_loads.append(load(n.wout.at[pl.ds(pl.multiple_of(at.h * E, 16), E)], n.wout_v))
    if aligned:
        first_loads.append(load(n.dattn.at[:, head_lanes], n.dcols_v))
    else:
        first_loads.append(load(n.dattn_cols, n.dcols_v))
    attend_loads = [load(getattr(n, k), getattr(n, k + "_v")) for k in ("keys", "values", "lkeys", "lvalues", "query")]
    norm_load = load(n.key_norm, n.norm_v)
    own_quarters = [load(n.fall.at[quarter(group(dz, 0), at.y)], n.fall_b.at[quarter(group(dz, 0), at.y)]) for dz in range(1, nz)]
    ffn_loads = [load(getattr(n, k), getattr(n, k + "_v")) for k in ("ffn", "dout", "act", "dhid")]
    ffn_loads.append(load(n.wup.at[:, pl.ds(pl.multiple_of(at.h * F, 128), F)], n.wup_v))
    ffn_loads.append(load(n.wdown.at[pl.ds(pl.multiple_of(at.h * F, 16), F)], n.wdown_v))
    key_load = load(n.wk, n.w_v.at[0])
    value_load = load(n.wv, n.w_v.at[1])
    media_load = load(n.media, n.media_v)
    lat_load = load(n.lat, n.lat_v)
    dres_load = load(n.dres, n.dres_v)

    greet(at.head_peers() + [(at.z * nx + at.x_peer(d), at.h) for d in range(1, nx)] + [(at.z_peer(d) * nx + at.x, at.h) for d in range(1, nz)])

    def y_send(src, dst):
        return [copies.put(src, dst, (at.r, at.y_peer(d) * nc + at.c)) for d in range(1, ny)]

    def x_send(src, dst):
        return [copies.put(src, dst, (at.z * nx + at.x_peer(d), at.h)) for d in range(1, nx)]

    x_quarters = []
    for dz in range(nz):
        block = quarter(group(dz, 0), at.y)
        x_quarters.append(x_send(n.fall.at[block], n.fall_b.at[block]))
    y_quarters = {}
    for dz in range(1, nz):
        block = quarter(group(dz, 0), at.y)
        y_quarters[dz, 0] = y_send(n.fall.at[block], n.fall_b.at[block])

    def spread(dz, dx):
        for copy in y_quarters[dz, dx]:
            copy.wait_recv()
        if nc == 1:
            return None
        block = group(dz, dx), pl.ds(pl.multiple_of(at.c * ny * L, 16), ny * L)
        return copies.put(n.fall_b.at[block], n.fall_b.at[block], partner)

    wide_tile = tile_of(D, 512)
    for copy in first_loads:
        copy.wait()
    n.dmixed[...] = mt(n.dattn_v[...], n.wout_v[...]).astype(BF)

    def put_part(w, z, tile):
        for x in range(nx):
            n.parts[w, x, z] = tile[x * B : (x + 1) * B].astype(BF)

    tiles_per_head = E // (nx * B) if E % (nx * B) == 0 else 0
    if tiles_per_head:
        for head in range(H):
            put_part(3, head, tm(n.mix_v[head], n.dcols_v[...]))
    else:
        whole = jnp.concatenate([n.mix_v[head] for head in range(H)], axis=-1)
        for z in range(nz):
            put_part(3, z, tm(whole[:, z * nx * B : (z + 1) * nx * B], n.dcols_v[...]))
    x_parts, z_parts = {}, {}

    def rs_start(w):
        x_parts[w] = [
            copies.put(n.parts.at[w, at.x_peer(d)], n.x_recv.at[w, d - 1], (at.z * nx + at.x_peer(d), at.h)) for d in range(1, nx)
        ]

    def rs_middle(w):
        for copy in x_parts[w]:
            copy.wait_recv()

        def step(z):
            total = n.parts[w, at.x, z].astype(F32)
            for d in range(1, nx):
                total = total + n.x_recv[w, d - 1, z].astype(F32)
            n.sums[w, z] = total.astype(BF)

        loop(nz, step)
        z_parts[w] = [
            copies.put(n.sums.at[w, at.z_peer(d)], n.z_recv.at[w, d - 1], (at.z_peer(d) * nx + at.x, at.h)) for d in range(1, nz)
        ]

    def rs_end(w):
        for copy in z_parts[w]:
            copy.wait_recv()
        total = n.sums[w, at.z].astype(F32)
        for d in range(1, nz):
            total = total + n.z_recv[w, d - 1].astype(F32)
        n.grad_v[w] = total

    rs_start(3)
    for copy in attend_loads:
        copy.wait()
    scale = 1.0 / math.sqrt(HEAD_DIM)

    def back_image(i):
        q_rows = pl.ds(pl.multiple_of(i * LR, 16), LR)
        m_rows = pl.ds(pl.multiple_of(i * pl_rows, 16), pl_rows)
        q_all, d_all = n.query_v[q_rows], n.dmixed[q_rows]
        k_all = jnp.concatenate([n.keys_v[k, m_rows] for k in range(H)] + [n.lkeys_v[q_rows]], axis=0)
        v_all = jnp.concatenate([n.values_v[k, m_rows] for k in range(H)] + [n.lvalues_v[q_rows]], axis=0)
        dq, dk, dv = [], [], []
        for j in range(E // HEAD_DIM):
            part = slice(j * HEAD_DIM, (j + 1) * HEAD_DIM)
            q, k, v, d = q_all[:, part], k_all[:, part], v_all[:, part], d_all[:, part]
            scores = mt(q, k) * scale
            powers = jnp.exp(scores - jnp.max(scores, axis=-1, keepdims=True))
            probs = powers * (1.0 / jnp.sum(powers, axis=-1, keepdims=True))
            d_probs = mt(d, v)
            inner = jnp.sum(probs * d_probs, axis=-1, keepdims=True)
            d_scores = (probs * (d_probs - inner)).astype(BF)
            dq.append(mm(d_scores, k) * scale)
            dk.append(tm(d_scores, q) * scale)
            dv.append(tm(probs.astype(BF), d))
        dq, dk, dv = [jnp.concatenate(p, axis=-1) for p in (dq, dk, dv)]
        for j, grad in enumerate((dk, dv)):
            for k in range(H):
                n.dkv[j, k, m_rows] = grad[k * pl_rows : (k + 1) * pl_rows].astype(BF)
        for j, grad in enumerate((dk[H * pl_rows :], dv[H * pl_rows :], dq)):
            for head in range(H):
                n.turn[j, head, pl.ds(pl.multiple_of(i * ll, 8), ll)] = grad[head * ll : (head + 1) * ll]

    loop(G, back_image)
    for k in range(H):
        head = head_of(k)
        n.dkv[0, k, M:ML] = n.turn[0, head].astype(BF)
        n.dkv[1, k, M:ML] = n.turn[1, head].astype(BF)
        n.dqs[k] = n.turn[2, head].astype(BF)
    turned = {}
    for d in range(ny):
        for e in range(nc):
            k = d * nc + e
            if k == 0:
                continue
            peer = (at.r, head_of(k))
            to = (ny - d) % ny * nc + e
            turned[to] = [copies.put(n.dkv.at[j, k], n.dkv_recv.at[j, to], peer) for j in range(2)]
            turned[to].append(copies.put(n.dqs.at[k], n.dqs_recv.at[to], peer))
    for copy in own_quarters:
        copy.wait()
    near_blocks = [spread(dz, 0) for dz in range(1, nz)]
    norm_load.wait()
    for w in (1, 2, 0):

        def tile_step(z):
            lanes = pl.ds(pl.multiple_of(z * nx * B, 128), nx * B)
            if w == 0:
                total = sum(tm(n.norm_v[k, M:ML, lanes], n.dqs[k]) for k in range(H))
            else:
                total = sum(tm(n.norm_v[k, :, lanes], n.dkv[w - 1, k]) for k in range(H))
            put_part(w, z, total)

        loop(nz, tile_step)
        rs_start(w)
    for dx in range(1, nx):
        for dz in range(nz):
            x_quarters[dz][dx - 1].wait_recv()
            block = quarter(group(dz, nx - dx), at.y)
            y_quarters[dz, nx - dx] = y_send(n.fall_b.at[block], n.fall_b.at[block])
    rs_middle(3)
    for copy in ffn_loads:
        copy.wait()
    base, offset = window_of(here, B, D)
    window = pl.ds(base, 256)
    hid_tile = 256

    def own_step(t):
        lanes = pl.ds(pl.multiple_of(t * hid_tile, 128), hid_tile)
        n.up_acc[:, lanes] = tm(n.ffn_v[:, window], n.dhid_v[:, lanes])
        n.down_acc[:, lanes] = tm(n.dout_v[:, window], n.act_v[:, lanes])

    loop(F // hid_tile, own_step)

    def other_group(dz, dx, arrival):
        for copy in arrival:
            if copy is not None:
                copy.wait_recv()
        r = group(dz, dx)
        loads = [load(n.fall_b.at[r], n.ffn_v), load(n.dall.at[r], n.dout_v)]
        for copy in loads:
            copy.wait()

        def step(t):
            lanes = pl.ds(pl.multiple_of(t * hid_tile, 128), hid_tile)
            value, slope = gelu_pair(mm(n.ffn_v[...], n.wup_v[:, lanes]))
            d_act = mt(n.dout_v[...], n.wdown_v[lanes, :])
            n.up_acc[:, lanes] += tm(n.ffn_v[:, window], (d_act * slope).astype(BF))
            n.down_acc[:, lanes] += tm(n.dout_v[:, window], value.astype(BF))

        loop(F // hid_tile, step)

    for dz in range(1, nz):
        other_group(dz, 0, [near_blocks[dz - 1]])
        if dz == 1:
            rs_middle(1)
    key_load.wait()
    value_load.wait()
    n.dkv_recv[0, 0] = n.dkv[0, 0]
    n.dkv_recv[1, 0] = n.dkv[1, 0]
    n.dqs_recv[0] = n.dqs[0]
    n.drow[...] = jnp.zeros((ML, D), F32)

    def back_rows(slot, rows_from, k, buf):
        def step(t):
            lanes = pl.ds(pl.multiple_of(t * wide_tile, 128), wide_tile)
            grad = n.dqs_recv[k] if slot == 2 else n.dkv_recv[slot, k]
            if aligned:
                weight = n.w_v[buf, lanes, pl.ds(pl.multiple_of(head_of(k) * E, 128), E)]
                n.drow[rows_from:ML, lanes] += mt(grad, weight)
            else:
                weight = n.w_v[buf, pl.ds(pl.multiple_of(head_of(k) * E, 16), E), lanes]
                n.drow[rows_from:ML, lanes] += mm(grad, weight)

        loop(D // wide_tile, step)

    slots = sorted(range(H), key=lambda k: (k >= nc, k))
    for k in slots:
        if k:
            turned[k][0].wait_recv()
        back_rows(0, 0, k, 0)
    query_load = load(n.wq, n.w_v.at[0])
    for k in slots:
        if k:
            turned[k][1].wait_recv()
        back_rows(1, 0, k, 1)
    query_load.wait()
    for k in slots:
        if k:
            turned[k][2].wait_recv()
        back_rows(2, M, k, 0)
    for copy in (media_load, lat_load, dres_load):
        copy.wait()
    n.vec[...] = jnp.zeros((4, 8, D), F32)

    def norm_back_rows(raw, rows, grad_rows, which, extra, out):
        hat, inv = norm_rows(raw[rows].astype(F32))
        grad = n.drow[grad_rows]
        n.vec[which] += jnp.sum((grad * hat).reshape(-1, 8, D), axis=0)
        n.vec[which + 1] += jnp.sum(grad.reshape(-1, 8, D), axis=0)
        scaled = grad * n.vecs[which : which + 1]
        first = jnp.mean(scaled, axis=-1, keepdims=True)
        second = jnp.mean(scaled * hat, axis=-1, keepdims=True)
        result = inv * (scaled - first - hat * second)
        out[grad_rows] = result if extra is None else result + extra[rows]

    def media_step(i):
        rows = pl.ds(pl.multiple_of(i * 32, 32), 32)
        norm_back_rows(n.media_v, rows, rows, 0, None, n.drow)

    loop(M // 32, media_step)

    def lat_step(i):
        rows = pl.ds(pl.multiple_of(i * 32, 32), 32)
        norm_back_rows(n.lat_v, rows, pl.ds(pl.multiple_of(M + i * 32, 32), 32), 2, n.dres_v, n.drow)

    loop(L // 32, lat_step)
    outs = [load(n.drow.at[0:M], n.media_o), load(n.drow.at[M:ML], n.lat_o)]
    n.vec_own[...] = jnp.concatenate(
        [jnp.sum(n.vec[i], axis=0, keepdims=True) for i in range(4)] + [n.fvec[0:2], jnp.zeros((2, D), F32)], axis=0
    )
    vec_head = [copies.put(n.vec_own, n.vec_head.at[k - 1], (at.r, lax.rem(at.h + k, H))) for k in range(1, H)]
    rs_middle(2)
    late_blocks = {}
    for dx in range(1, nx):
        for dz in range(nz):
            late_blocks[dz, dx] = spread(dz, dx)
    span = D // nz
    for i, (dz, dx) in enumerate(late_blocks):
        other_group(dz, dx, [late_blocks[dz, dx]])
        if i == 0:
            rs_middle(0)
            for copy in vec_head:
                copy.wait_recv()
            total = n.vec_own[...]
            for k in range(1, H):
                total = total + n.vec_head[k - 1]
            for z in range(nz):
                n.vec_sum[z] = total[:, z * span : (z + 1) * span]
            vec_z = [
                copies.put(n.vec_sum.at[at.z_peer(d)], n.vec_z.at[d - 1], (at.z_peer(d) * nx + at.x, at.h)) for d in range(1, nz)
            ]
        if i == 1:
            for copy in vec_z:
                copy.wait_recv()
            total = n.vec_sum[at.z]
            for d in range(1, nz):
                total = total + n.vec_z[d - 1]
            n.vec_part[...] = total
            vec_x = [
                copies.put(n.vec_part, n.vec_x.at[d - 1], (at.z * nx + at.x_peer(d), at.h)) for d in range(1, nx)
            ]
    outs += [load(n.up_acc, n.up_o), load(n.down_acc, n.down_o)]
    for w in (3, 1, 2, 0):
        rs_end(w)
        outs.append(load(n.grad_v.at[w], n.grads_o.at[w]))
    for copy in vec_x:
        copy.wait_recv()
    total = n.vec_part[...]
    for d in range(1, nx):
        total = total + n.vec_x[d - 1]
    n.vec_done[...] = total
    outs.append(load(n.vec_done, n.vec_o))
    copies.finish()
    for copy in outs:
        copy.wait()


def backward(s, a, media, lat, vecs, wq, wk, wv, wout, wup, wdown, dattn_cols):
    ny, nc = factor_head(s.heads)
    nz, nx = factor_rows(s.rows)
    G, L, D, E, F, H = s.images, s.images * s.lat, s.width, s.cols, s.mine, s.heads
    M, GL = s.images * s.patch, s.images * s.lat * s.heads
    ML, B = M + L, s.width // s.rows
    outs = dict(
        media_o=((M, D), F32), lat_o=((L, D), F32), grads_o=((4, B, E), F32), up_o=((256, F), F32), down_o=((256, F), F32),
        vec_o=((8, D // nz), F32), fall_b=((s.rows, GL, D), BF),
    )
    scratch = dict(
        dattn_v=((GL, D), BF), mix_v=((H, GL, E), BF), wout_v=((E, D), BF), dcols_v=((GL, E), BF), dmixed=((GL, E), BF),
        keys_v=((H, M, E), BF), values_v=((H, M, E), BF), lkeys_v=((GL, E), BF), lvalues_v=((GL, E), BF), query_v=((GL, E), BF),
        norm_v=((H, ML, D), BF), ffn_v=((GL, D), BF), dout_v=((GL, D), BF), act_v=((GL, F), BF), dhid_v=((GL, F), BF),
        wup_v=((D, F), BF), wdown_v=((F, D), BF), w_v=((2, D, D), BF), media_v=((M, D), BF), lat_v=((L, D), BF), dres_v=((L, D), F32),
        dkv=((2, H, ML, E), BF), dqs=((H, L, E), BF), turn=((3, H, L, E), F32), dkv_recv=((2, H, ML, E), BF), dqs_recv=((H, L, E), BF),
        parts=((4, nx, nz, B, E), BF), x_recv=((4, max(nx - 1, 1), nz, B, E), BF), sums=((4, nz, B, E), BF),
        z_recv=((4, max(nz - 1, 1), B, E), BF), grad_v=((4, B, E), F32), up_acc=((256, F), F32), down_acc=((256, F), F32),
        drow=((ML, D), F32), vec=((4, 8, D), F32), vec_own=((8, D), F32), vec_head=((max(H - 1, 1), 8, D), F32),
        vec_sum=((nz, 8, D // nz), F32), vec_z=((max(nz - 1, 1), 8, D // nz), F32), vec_part=((8, D // nz), F32),
        vec_x=((max(nx - 1, 1), 8, D // nz), F32), vec_done=((8, D // nz), F32),
    )
    ins = dict(
        media=media, lat=lat, vecs=vecs, fvec=a["fvec_o"], dres=a["dres_o"], key_norm=a["key_norm_o"], keys=a["keys_o"],
        values=a["values_o"], lkeys=a["lkeys_o"], lvalues=a["lvalues_o"], query=a["query_o"], mixed=a["mixed_o"], dattn=a["dattn_o"],
        ffn=a["ffn_o"], dout=a["dout_o"], act=a["act_o"], dhid=a["dhid_o"], dall=a["dall"], fall=a["fall"], wq=wq, wk=wk, wv=wv,
        wout=wout, wup=wup, wdown=wdown,
    )
    if dattn_cols is not None:
        ins["dattn_cols"] = dattn_cols
    vmem = pl.BlockSpec(memory_space=pltpu.VMEM)
    s.names = list(ins) + list(outs) + list(scratch) + ["send", "recv", "local"]
    result = pl.pallas_call(
        functools.partial(backward_kernel, s),
        name="backward",
        out_shape=[jax.ShapeDtypeStruct(*o) for o in outs.values()],
        in_specs=[vmem if k in ("vecs", "fvec") else ANY for k in ins],
        out_specs=[ANY] * len(outs),
        scratch_shapes=[pltpu.VMEM(*v) for v in scratch.values()]
        + [pltpu.SemaphoreType.DMA((300,)), pltpu.SemaphoreType.DMA((300,)), pltpu.SemaphoreType.DMA((100,))],
        compiler_params=pltpu.CompilerParams(collective_id=2, has_side_effects=True, vmem_limit_bytes=62 << 20),
        cost_estimate=pl.CostEstimate(flops=30 * 10**9, bytes_accessed=8 * 10**7, transcendentals=10**6),
    )(*ins.values())
    return dict(zip(outs, result, strict=True))


def body(
    media, latents, counts, media_gain, media_shift, latent_gain, latent_shift, w_query, w_key, w_value, w_out,
    ffn_gain, ffn_shift, w_up, w_down, cotangent,
):
    rows, heads = lax.axis_size("rows"), lax.axis_size("head")
    at = Place(rows, heads)
    images, patch, width = media.shape
    lat = latents.shape[1]
    cols = width // heads
    s = types.SimpleNamespace(
        rows=rows, heads=heads, images=images, patch=patch, lat=lat, width=width, cols=cols, mine=w_up.shape[1] // heads
    )
    ids = at.r * images + jnp.arange(images, dtype=jnp.int32)
    table = jnp.arange(counts.shape[0], dtype=jnp.int32)
    limit = jnp.sum(jnp.where((ids // MAX_IMG)[:, None] == table[None, :], counts[None, :], 0), axis=1)
    live = ((ids % MAX_IMG) < limit).astype(F32)
    mask = jnp.repeat(live, lat)[:, None]
    vecs = jnp.stack([media_gain, media_shift, latent_gain, latent_shift, ffn_gain, ffn_shift, ffn_gain, ffn_shift])
    aligned = cols % 128 == 0

    def columns(array):
        return array if aligned else lax.dynamic_slice_in_dim(array, at.h * cols, cols, 1)

    flat_media, flat_lat, flat_cot = media.reshape(-1, width), latents.reshape(-1, width), cotangent.reshape(-1, width)
    a = forward(
        s, flat_media, flat_lat, flat_cot, mask, vecs, columns(w_query), columns(w_key), columns(w_value), w_out, w_up, w_down
    )
    turned = [w if aligned else w.T for w in (w_query, w_key, w_value)]
    b = backward(s, a, flat_media, flat_lat, vecs, *turned, w_out, w_up, w_down, None if aligned else columns(a["dattn_o"]))
    block = width // rows
    _, offset = window_of(at.r, block, width)
    up_grad = lax.dynamic_slice_in_dim(b["up_o"], offset, block, 0)
    down_grad = lax.dynamic_slice_in_dim(b["down_o"], offset, block, 0).T
    share = width // (rows * heads)
    vector = lax.dynamic_slice_in_dim(b["vec_o"], (at.x * heads + at.h) * share, share, 1)
    grads = b["grads_o"]
    return (
        a["out_o"].reshape(latents.shape), b["media_o"].reshape(media.shape), b["lat_o"].reshape(latents.shape),
        vector[0], vector[1], vector[2], vector[3], grads[0], grads[1], grads[2], grads[3], vector[4], vector[5], up_grad, down_grad,
    )


def solution(mesh):
    row = P("rows", "head", None)
    whole = P()
    vector = P(("rows", "head"))
    grid = P("rows", "head")
    return jax.shard_map(
        body,
        mesh=mesh,
        in_specs=(row, row) + (whole,) * 13 + (row,),
        out_specs=(row, row, row, vector, vector, vector, vector, grid, grid, grid, grid, vector, vector, grid, P("head", "rows")),
        check_vma=False,
    )
```

time: 506 us -> 232 us (0.46); the launches traced: 497 us -> 231 us
  matrix products: 106 us -> 0 us
  other arithmetic: 68.4 us -> 0.86 us
  waiting for transfers between devices: 41.5 us -> 0 us
  local copies, waits for them, and re-layouts: 51.2 us -> 15.2 us
  starting transfers between devices: 16.6 us -> 0 us
    dot_general x18 -> x0, matrix products: 106 us -> none  [dot(): return lax.dot_general(a, b, (dims, ((), ())), preferred_element_type=F32)]
    ppermute x16 -> x0, waiting for transfers between devices: 41.5 us -> none  [the longest x8 26.1 us: gather_rows(): lax.ppermute(block, 'rows', [(z * nx + x, z * nx + (x + d) % nx) for z in...]
    ppermute x16 -> x0, starting transfers between devices: 16.6 us -> none  [the longest x6 9.3 us: gather_rows(): lax.ppermute(part, 'rows', [(z * nx + x, (z + d) % nz * nx + x) for z in...]
    convert_element_type x10 -> x1, other arithmetic: 16.5 us -> 0.01 us  [body(): live = (ids % MAX_IMG < limit).astype(F32)]
    reshape x9 -> x0, local copies, waits for them, and re-layouts: 15.2 us -> none  [the longest x4 5.97 us: body(): p.astype(BF).reshape(nz, nx, block, cols)]
    reduce_sum x20 -> x1, other arithmetic: 15.2 us -> 0.84 us  [body(): jnp.sum(jnp.where((ids // MAX_IMG)[:, None] == table[None, :], counts[Non...]
    add x9 -> x0, other arithmetic: 12.1 us -> none  [the longest x4 6.73 us: body(): lax.dynamic_index_in_dim(s, at.z, 0, keepdims=False).astype(F32)]
    unnamed x148 -> x11, local copies, waits for them, and re-layouts: 14.8 us -> 2.73 us
  transfers between devices with their start and end apart: 16 -> 0, of which waited for: 3 -> 0; matrix products, arithmetic and copies ran while one was open for 31% -> 0% of each run, Pallas kernels for 31% -> 0%
where the time goes in v2:
time: 232 us; the launch traced here: 231 us
  Pallas kernels  214 us (92%)
  local copies, waits for them, and re-layouts  15.2 us (7%)
    pallas_call x1, Pallas kernels, backward(): pl.pallas_call(functools.partial(backward_kernel, s), name='backward', ou...  126 us
    pallas_call x1, Pallas kernels, forward(): pl.pallas_call(functools.partial(forward_kernel, s), name='forward', out_...  88.3 us
    another operation x7, local copies, waits for them, and re-layouts, body(): jnp.stack([media_gain, media_shift, latent_gain, latent_shift, ffn_gain,...  4.9 us

profile of v2, /device:TPU:0, one launch (start us, length us, event | category | flops | bytes accessed | tf_op | source)
XLA Modules:
  0.0 230.7 jit_solution(11237195082060944415)
XLA Ops:
  0.7 0.8 select_reduce_fusion
  1.6 0.1 broadcast_in_dim.20
  1.6 0.7 stack.23
  2.3 0.7 stack.24
  3.0 0.7 stack.25
  3.7 0.7 stack.26
  4.4 0.7 stack.27
  5.1 0.7 stack.28
  5.8 0.7 stack.29.refs_4_.refs_2_
  6.5 0.7 broadcast_in_dim_reshape.4.refs_3_
  7.2 88.3 %forward.1 = (f32[64,1536]{1,0:T(8,128)}, f32[64,1536]{1,0:T(8,128)}, f32[8,1536]{1,0:T(8,128)}, bf16[4,320,1536]{2,1,0:T(8,128)(2,1)}, bf16[4,256,384]{2,1,0:T(...) custom-call(bf16[256,1536]{1,0:T(8,128)(2,1)} %bitcast.29, ...), custom_call_target="tpu_custom_call" | custom-call | flops 8000000000 | bytes 40000000 | tf_op jit(solution)/shard_map/forward/pallas_call | solution.py:569
  95.5 125.6 %backward.1 = (f32[256,1536]{1,0:T(8,128)}, f32[64,1536]{1,0:T(8,128)}, f32[4,192,384]{2,1,0:T(8,128)}, f32[256,1536]{1,0:T(8,128)}, f32[256,1536]{1,0:T(8,128)}...) custom-call(bf16[256,1536]{1,0:T(8,128)(2,1)} %bitcast.30, bf16[64,1536]{1,0:T(8,128)(2,1)} %bitcast.35, ...), custom_call_target="tpu_custom_call" | custom-call | flops 30000001024 | bytes 80000000 | tf_op jit(solution)/shard_map/backward/pallas_call | solution.py:958
  221.2 0.0 copy-start.1
  221.2 0.9 constant_dynamic-slice_fusion.1
  222.1 0.5 slice_bitcast_fusion.4
  222.6 2.3 slice_bitcast_fusion
  224.9 0.0 copy-done.1
  224.9 0.0 copy-start.2
  224.9 0.0 copy-start
  224.9 3.1 %dynamic-slice_bitcast_fusion = (f32[1536,192]{0,1:T(8,128)}, f32[192,1536]{1,0:T(8,128)}) fusion(f32[256,1536]{1,0:T(8,128)} %get-tuple-element.60, s32[]{:T(128)S(6)} %select_n.43, f32[256,1536]{1,0:T(8,128)S(1)} %copy-done.1), kind=kLoop, calls=%fused_computation | loop fusion | bytes 4718596 | tf_op jit(solution)/shard_map/transpose | solution.py:1004
  228.0 0.0 copy-done.2
  228.0 0.7 copy.36
  228.7 0.0 copy-done
  228.7 0.0 copy-start.3
  228.7 1.1 copy.37
  229.9 0.1 copy-done.3
  230.0 0.7 copy.38
  (2 shorter events, 0.0 us)
Async XLA Ops:
  221.2 3.7 %copy-start.1 = (f32[256,1536]{1,0:T(8,128)S(1)}, f32[256,1536]{1,0:T(8,128)}, u32[]{:S(2)}) copy-start(f32[256,1536]{1,0:T(8,128)} %get-tuple-element.59) | copy-start | bytes 4718596
  224.9 3.1 %copy-start.2 = (f32[64,1536]{1,0:T(8,128)S(1)}, f32[64,1536]{1,0:T(8,128)}, u32[]{:S(2)}) copy-start(f32[64,1536]{1,0:T(8,128)} %get-tuple-element.38) | copy-start | bytes 1179652
  224.9 3.8 %copy-start = (f32[256,1536]{1,0:T(8,128)S(1)}, f32[256,1536]{1,0:T(8,128)}, u32[]{:S(2)}) copy-start(f32[256,1536]{1,0:T(8,128)} %get-tuple-element.55) | copy-start | bytes 4718596
  228.7 1.2 copy-start.3
